TPU v7x, 768 devices: a whole 4x8x12 slice. The times are simulated.
768 devices in a mesh: dp: 24 (over x_hi, z), graph: 32 (over x_lo, y, core).
Axes of the slice: x: 4 (x_hi: 2, x_lo: 2; x = x_hi * 2 + x_lo), y: 8, z: 12, core: 2. Of those that a mesh axis runs over, the one named last changes fastest.
Arguments:
- atom_h: bfloat16 [24, 256, 1024], P('dp', 'graph'), may hold values from -6 to 6
- edge_x: bfloat16 [24, 16384, 1024], P('dp', 'graph'), may hold values from -6 to 6
- edge_source: int32 [24, 16384], P('dp', 'graph'), may hold values from 0 to 255, as said below
- edge_target: int32 [24, 16384], P('dp', 'graph'), may hold values from 0 to 255, as said below
- trip_in: int32 [24, 32768], P('dp', 'graph'), may hold values from 0 to 16383, as said below
- trip_out: int32 [24, 32768], P('dp', 'graph'), may hold values from 0 to 16383, as said below
- basis: bfloat16 [24, 64, 32768], P('dp', None, 'graph'), may hold values from -6 to 6
- block_counts: int32 [24, 32], P('dp', 'graph'), may hold values from 2 to 8, as said below
- atom_cotangent: bfloat16 [24, 256, 1024], P('dp', 'graph'), may hold values from -6 to 6
- weight_edge: bfloat16 [1024, 1024], replicated, may hold values from -0.1875 to 0.1875
- weight_basis: bfloat16 [64, 1024], replicated, may hold values from -0.75 to 0.75
Outputs:
- grad_x: bfloat16 [24, 16384, 1024], P('dp', 'graph')
- grad_h: bfloat16 [24, 256, 1024], P('dp', 'graph')
- grad_weight_edge: float32 [1024, 1024], P('graph')
- grad_weight_basis: float32 [64, 1024], P(None, 'graph')
Inputs may be any that keep to these rules, and one draw needn't show every extreme that they name: `edge_source`: the source atom of an edge may be any atom of its graph batch. `edge_target`: the target atom of an edge belongs to the edge's own device (edges g * 512 onward, atoms g * 8 onward). `trip_in`: every triplet slot of device g names an edge of device g. `trip_out`: every triplet slot of device g names an edge of device g. `block_counts`: in every batch some device uses all 8 blocks.
All inputs are finite; a program needn't handle non-finite values.
Results may differ from a plain program's by a relative error of at most 0.0074.
Values may be sent and summed in bfloat16 or wider, within the bound.
A program may use at most 32 MiB of HBM per device.

v0:
```python
import jax
import jax.numpy as jnp
from jax import lax
from jax.sharding import PartitionSpec as P

BLOCK = 128


def silu_slope(pre):
    logistic = jax.nn.sigmoid(pre)
    return logistic * (1.0 + pre * (1.0 - logistic))


def shards(
    atom_h,
    edge_x,
    edge_source,
    edge_target,
    trip_in,
    trip_out,
    basis,
    block_counts,
    atom_cotangent,
    weight_edge,
    weight_basis,
):
    hrows = atom_h[0]
    xrows = edge_x[0]
    cotan = atom_cotangent[0]
    bas = basis[0]
    atoms_dev = hrows.shape[0]
    edges_dev = xrows.shape[0]
    width = xrows.shape[1]
    groups = lax.axis_size("graph")
    total_atoms = atoms_dev * groups
    where_dev = lax.axis_index("graph")
    edge_base = where_dev * edges_dev
    atom_base = where_dev * atoms_dev
    target_local = edge_target[0] - atom_base
    source = edge_source[0]
    table = lax.all_gather(hrows, "graph", axis=0, tiled=True)
    source_rows = jnp.take(table, source, axis=0).astype(jnp.float32)
    joined = (
        xrows.astype(jnp.float32)
        + source_rows
        + jnp.take(hrows, target_local, axis=0).astype(jnp.float32)
    ).astype(jnp.bfloat16)
    pre = jnp.dot(joined, weight_edge, preferred_element_type=jnp.float32)
    message = jax.nn.silu(pre).astype(jnp.bfloat16)
    spread = lax.dot_general(
        bas, weight_basis, (((0,), (0,)), ((), ())), preferred_element_type=jnp.float32
    ).astype(jnp.bfloat16)
    edge_grad = jnp.take(cotan, target_local, axis=0)
    tin_local = trip_in[0] - edge_base
    tout_local = trip_out[0] - edge_base
    edge_ids = jnp.arange(edges_dev, dtype=jnp.int32)

    def one_block(block, carry):
        grad_message, grad_wb = carry
        begin = block * BLOCK
        tin = lax.dynamic_slice_in_dim(tin_local, begin, BLOCK, 0)
        tout = lax.dynamic_slice_in_dim(tout_local, begin, BLOCK, 0)
        spread_block = lax.dynamic_slice_in_dim(spread, begin, BLOCK, 0)
        basis_block = lax.dynamic_slice_in_dim(bas, begin, BLOCK, 1)
        out_grad = jnp.take(edge_grad, tout, axis=0).astype(jnp.float32)
        grad_msg = (spread_block.astype(jnp.float32) * out_grad).astype(jnp.bfloat16)
        grad_spread = (jnp.take(message, tin, axis=0).astype(jnp.float32) * out_grad).astype(
            jnp.bfloat16
        )
        incidence = (edge_ids[:, None] == tin[None, :]).astype(jnp.bfloat16)
        grad_message = grad_message + jnp.dot(
            incidence, grad_msg, preferred_element_type=jnp.float32
        )
        grad_wb = grad_wb + jnp.dot(basis_block, grad_spread, preferred_element_type=jnp.float32)
        return (grad_message, grad_wb)

    start_carry = (
        jnp.zeros((edges_dev, width), jnp.float32),
        jnp.zeros((bas.shape[0], width), jnp.float32),
    )
    grad_message, grad_wb = lax.fori_loop(0, block_counts[0, 0], one_block, start_carry)
    grad_pre = (grad_message * silu_slope(pre)).astype(jnp.bfloat16)
    grad_x = lax.dot_general(
        grad_pre, weight_edge, (((1,), (1,)), ((), ())), preferred_element_type=jnp.float32
    ).astype(jnp.bfloat16)
    grad_w = lax.dot_general(
        joined, grad_pre, (((0,), (0,)), ((), ())), preferred_element_type=jnp.float32
    )
    share_w, share_wb = (
        lax.psum_scatter(grad_w, "graph", scatter_dimension=0, tiled=True),
        lax.psum_scatter(grad_wb, "graph", scatter_dimension=1, tiled=True),
    )
    total_w, total_wb = lax.psum((share_w, share_wb), "dp")
    own_ids = jnp.arange(atoms_dev, dtype=jnp.int32)
    target_hits = (own_ids[:, None] == target_local[None, :]).astype(jnp.bfloat16)
    target_part = jnp.dot(target_hits, grad_x, preferred_element_type=jnp.float32)
    all_ids = jnp.arange(total_atoms, dtype=jnp.int32)
    source_hits = (all_ids[:, None] == source[None, :]).astype(jnp.bfloat16)
    source_part = jnp.dot(source_hits, grad_x, preferred_element_type=jnp.float32)
    source_own = lax.psum_scatter(source_part, "graph", scatter_dimension=0, tiled=True)
    grad_h = (cotan.astype(jnp.float32) + source_own + target_part).astype(jnp.bfloat16)
    return (grad_x[None], grad_h[None], total_w, total_wb)


def solution(mesh):
    placed = (
        P("dp", "graph", None),
        P("dp", "graph", None),
        P("dp", "graph"),
        P("dp", "graph"),
        P("dp", "graph"),
        P("dp", "graph"),
        P("dp", None, "graph"),
        P("dp", "graph"),
        P("dp", "graph", None),
        P(),
        P(),
    )
    return jax.shard_map(
        shards,
        mesh=mesh,
        in_specs=placed,
        out_specs=(
            P("dp", "graph", None),
            P("dp", "graph", None),
            P("graph", None),
            P(None, "graph"),
        ),
        check_vma=False,
    )
```

profile of v0, /device:TPU:6, one launch (start us, length us, event | category | flops | bytes accessed | tf_op | source)
XLA Modules:
  0.0 770.0 jit_solution(5325080640692970006)
XLA Ops:
  9.5 35.8 %all-gather = bf16[1,256,1024]{2,1,0:T(8,128)(2,1)S(1)} all-gather(bf16[1,8,1024]{2,1,0:T(8,128)(2,1)} %param.17), channel_id=2, replica_groups=mesh['dp'=24,'graph'=32] {'graph'}, dimensions={1}, use_global_device_ids=true | all-gather | bytes 540672 | tf_op jit(solution)/shard_map/all_gather | solution.py:41
  45.2 2.8 gather_fusion.4
  48.0 2.8 gather_fusion.3
  50.8 2.8 gather_fusion.2
  53.6 1.5 broadcast_select_fusion.3
  55.2 2.0 convolution_convert_fusion
  57.9 3.1 multiply_convert_fusion.1
  62.3 1.6 broadcast_in_dim.45
  63.9 92.2 %while.13 = (s32[]{:T(128)}, f32[512,1024]{1,0:T(8,128)}, f32[64,1024]{1,0:T(8,128)}, s32[]{:T(128)}, s32[1024]{0:T(1024)}, /*index=5*/bf16[1024,1024]{1,0:T(8,1...) while((s32[]{:T(128)}, f32[512,1024]{1,0:T(8,128)}, ...), condition=%wide.region_1.0_spmd.clone, body=%wide.region_0.3_spmd.clone.sunk | while | flops 153096064 | bytes 6849243 | solution.py:81
  64.6 1.4 compare_and_fusion.5
  68.1 3.2 gather_fusion.1
  71.4 2.1 convolution_add_fusion.6
  73.4 3.6 convolution_add_fusion.5
  77.7 1.4 compare_and_fusion.5
  81.2 3.2 gather_fusion.1
  84.5 2.1 convolution_add_fusion.6
  86.5 3.6 convolution_add_fusion.5
  90.8 1.4 compare_and_fusion.5
  94.3 3.2 gather_fusion.1
  97.5 2.1 convolution_add_fusion.6
  99.6 3.6 convolution_add_fusion.5
  103.8 1.4 compare_and_fusion.5
  107.4 3.2 gather_fusion.1
  110.6 2.1 convolution_add_fusion.6
  112.7 3.6 convolution_add_fusion.5
  116.9 1.4 compare_and_fusion.5
  120.5 3.2 gather_fusion.1
  123.7 2.1 convolution_add_fusion.6
  125.8 3.6 convolution_add_fusion.5
  130.0 1.4 compare_and_fusion.5
  133.6 3.2 gather_fusion.1
  136.8 2.1 convolution_add_fusion.6
  138.9 3.6 convolution_add_fusion.5
  146.7 3.2 gather_fusion.1
  149.9 2.1 convolution_add_fusion.6
  151.9 3.6 convolution_add_fusion.5
  156.2 1.9 copy.16
  158.2 3.0 multiply_convert_fusion
  162.2 3.3 fusion.24
  165.6 2.5 convolution_convert_fusion.1
  168.2 1.4 fusion.20
  169.7 122.6 %reduce-scatter.8.cloned.1.call-done = f32[64,32]{0,1:T(8,128)} async-done(((f32[64,1024]{0,1:T(8,128)}), f32[64,32]{0,1:T(8,128)}) %reduce-scatter.8.cloned.1.call-update) | async-done | bytes 8208 | tf_op jit(solution)/shard_map/reduce_scatter | solution.py:91
  292.2 113.8 %psum.15 = f32[64,32]{0,1:T(8,128)} all-reduce(f32[64,32]{0,1:T(8,128)} %reduce-scatter.8.cloned.1.call-done), channel_id=1, replica_groups=mesh['dp'=24,'graph'=32] {'dp'}, use_global_device_ids=true, to_apply=%region_6.9 | all-reduce | flops 2048 | bytes 16384 | tf_op jit(solution)/shard_map/psum | solution.py:93
  406.0 14.2 %reduce-scatter.6.cloned.1.call-done = f32[32,1024]{1,0:T(8,128)} async-done(((f32[1024,1024]{1,0:T(8,128)}), f32[32,1024]{1,0:T(8,128)}) %reduce-scatter.6.cloned.1.call-update) | async-done | bytes 131088 | tf_op jit(solution)/shard_map/reduce_scatter | solution.py:90
  420.3 120.1 %reduce-scatter.4.cloned.1.call-done = f32[8,1024]{1,0:T(8,128)} async-done(((f32[256,1024]{1,0:T(8,128)}), f32[8,1024]{1,0:T(8,128)}) %reduce-scatter.4.cloned.1.call-update) | async-done | bytes 32784 | tf_op jit(solution)/shard_map/reduce_scatter | solution.py:100
  540.4 1.6 fusion.19
  542.0 219.9 %all-reduce.2.cloned.1.call-done = f32[32,1024]{1,0:T(8,128)} async-done(((f32[32,1024]{1,0:T(8,128)}), f32[32,1024]{1,0:T(8,128)}) %all-reduce.2.cloned.1.call-update) | async-done | bytes 131088 | tf_op jit(solution)/shard_map/psum | solution.py:93
  761.9 1.6 copy.27
  (95 shorter events, 22.1 us)
Async XLA Ops:
  7.2 50.7 %copy-start = (bf16[1024,1024]{1,0:T(8,128)(2,1)S(1)}, bf16[1024,1024]{1,0:T(8,128)(2,1)}, u32[]{:S(2)}) copy-start(bf16[1024,1024]{1,0:T(8,128)(2,1)} %param.26) | copy-start | bytes 6291460
  7.2 38.1 %copy-start.1 = (bf16[1,8,1024]{2,1,0:T(8,128)(2,1)S(1)}, bf16[1,8,1024]{2,1,0:T(8,128)(2,1)}, u32[]{:S(2)}) copy-start(bf16[1,8,1024]{2,1,0:T(8,128)(2,1)} %param.17) | copy-start | bytes 49156
  7.2 285.0 %reduce-scatter.8.cloned.1.call-start = ((), (), s32[]{:S(2)}) async-start(), calls=%async_computation.6 | async-start | bytes 540672 | tf_op jit(solution)/shard_map/reduce_scatter | solution.py:91
  8.1 37.2 %copy-start.13 = (s32[1,512]{1,0:T(1,128)}, s32[1,512]{1,0:T(1,128)S(1)}, u32[]{:S(2)}) copy-start(s32[1,512]{1,0:T(1,128)S(1)} %broadcast_subtract_fusion.2) | copy-start | bytes 6148
  45.2 2.8 copy-start.2
  50.8 4.4 copy-start.10
  50.8 4.4 copy-start.11
  53.6 3.6 copy-start.5
  53.6 3.6 copy-start.6
  53.6 3.6 copy-start.9
  57.8 3.1 copy-start.3
  57.8 3.1 copy-start.16
  57.9 3.1 copy-start.17
  66.0 0.6 copy-start.12
  79.0 0.6 copy-start.12
  92.1 0.6 copy-start.12
  105.2 0.6 copy-start.12
  118.3 0.6 copy-start.12
  131.4 0.6 copy-start.12
  144.5 0.6 copy-start.12
  158.1 262.1 %reduce-scatter.6.cloned.1.call-start = ((), (), s32[]{:S(2)}) async-start(), calls=%async_computation.4 | async-start | bytes 4325376 | tf_op jit(solution)/shard_map/reduce_scatter | solution.py:90
  158.2 4.0 copy-start.4
  161.2 1.0 copy-start.8
  165.5 2.6 copy-start.15
  165.6 374.8 %reduce-scatter.4.cloned.1.call-start = ((), (), s32[]{:S(2)}) async-start(), calls=%async_computation.3 | async-start | bytes 1081344 | tf_op jit(solution)/shard_map/reduce_scatter | solution.py:100
  168.1 373.9 %copy-start.7 = (bf16[512,1024]{1,0:T(8,128)(2,1)}, bf16[512,1024]{1,0:T(8,128)(2,1)S(1)}, u32[]{:S(2)}) copy-start(bf16[512,1024]{1,0:T(8,128)(2,1)S(1)} %convolution_convert_fusion.1) | copy-start | bytes 3145732
  168.1 372.2 %copy-start.14 = (s32[1,512]{1,0:T(1,128)S(1)}, s32[1,512]{1,0:T(1,128)}, u32[]{:S(2)}) copy-start(s32[1,512]{1,0:T(1,128)} %copy-done.13) | copy-start | bytes 6148
  169.6 592.3 %all-reduce.2.cloned.1.call-start = ((), (), s32[]{:S(2)}) async-start(), calls=%async_computation.5 | async-start | bytes 262144 | tf_op jit(solution)/shard_map/psum | solution.py:93
Sparse Core Ops, SparseCore 0:
  158.3 133.9 reduce-scatter.7
  295.6 124.5 reduce-scatter.5
  423.7 116.6 reduce-scatter.3
  543.4 218.4 all-reduce.1
where the time goes:
time: 772 us; the launch traced here: 770 us
  waiting for transfers between devices  477 us (62%)
  blocking collectives  150 us (19%)
  matrix products  53.4 us (7%)
  local copies, waits for them, and re-layouts  44.7 us (6%)
  other arithmetic  26.1 us (3%)
  between operations  14 us (2%)
    psum x1, waiting for transfers between devices, shards(): total_w, total_wb = lax.psum((share_w, share_wb), 'dp')  220 us
    reduce_scatter x1, waiting for transfers between devices, shards(): lax.psum_scatter(grad_wb, 'graph', scatter_dimension=1, tiled=True)  123 us
    reduce_scatter x1, waiting for transfers between devices, shards(): lax.psum_scatter(source_part, 'graph', scatter_dimension=0, tiled=True)  120 us
    psum x1, blocking collectives, shards(): total_w, total_wb = lax.psum((share_w, share_wb), 'dp')  114 us
    all_gather x1, blocking collectives, shards(): table = lax.all_gather(hrows, 'graph', axis=0, tiled=True)  35.8 us
    dot_general x7, matrix products, one_block(): jnp.dot(incidence, grad_msg, preferred_element_type=jnp.float32)  25 us
    gather x7, local copies, waits for them, and re-layouts, one_block(): jnp.take(message, tin, axis=0).astype(jnp.float32) * out_grad  22.5 us
  transfers between devices with their start and end apart: 4, of which 4 were waited for; matrix products, arithmetic and copies ran while one was open for 2% of the time, Pallas kernels for 0%

commit v1 on v0

v1 whole, which is shorter than its diff:
```python
import jax
import jax.numpy as jnp
from jax import lax
from jax.experimental import pallas as pl
from jax.experimental.pallas import tpu as pltpu
from jax.sharding import PartitionSpec as P

BLOCK = 128
NX, NY, NC = 2, 8, 2
MESH = pl.DeviceIdType.MESH
F32 = jnp.float32
BF16 = jnp.bfloat16
TN = (((0,), (0,)), ((), ()))
NT = (((1,), (1,)), ((), ()))
DIST = (4, 3, 3, 2, 2, 1, 1)
HALF = (0, 1, 0, 1, 0, 1, 0)
ORDER = (4, 3, 5, 2, 6, 1, 7, 0)


def dot(a, b, dims=None):
    if dims is None:
        return jnp.dot(a, b, preferred_element_type=F32)
    return lax.dot_general(a, b, dims, preferred_element_type=F32)


def kernel(
    n_dp,
    h_ref,
    x_hbm,
    src_ref,
    tgt_ref,
    tin_ref,
    tout_ref,
    basis_ref,
    counts_ref,
    cot_ref,
    we_hbm,
    wb_ref,
    gx_hbm,
    gh_ref,
    gw_ref,
    gwb_ref,
    x_ref,
    we_ref,
    table,
    tab,
    mt_ref,
    g_ref,
    gm_ref,
    joined_ref,
    gp_ref,
    gx_ref,
    part,
    from_core,
    from_left,
    from_right,
    acc,
    x_out,
    x_in,
    dp_out,
    dp_in,
    dp_all,
    load_sem,
    ag_send,
    ag_recv,
    sib_send,
    sib_recv,
    core_send,
    core_recv,
    left_send,
    left_recv,
    right_send,
    right_recv,
    pair_send,
    pair_recv,
    dps_send,
    dps_recv,
    dpg_send,
    dpg_recv,
):
    edges, width = x_ref.shape
    nb, trips = basis_ref.shape
    atoms_dev = h_ref.shape[0]
    half = width // 2
    wcols = 2 * width
    bcols = wcols + 128
    cols = bcols + half
    blocks = bcols // 128
    chips = NX * NY
    dp = lax.axis_index("dp")
    g = lax.axis_index("graph")
    chip = lax.div(g, NC)
    c = lax.rem(g, NC)
    xl = lax.div(chip, NY)
    y = lax.rem(chip, NY)
    oc = 1 - c
    sibling = {"graph": chip * NC + oc}
    right = {"graph": (xl * NY + lax.rem(y + 1, NY)) * NC + c}
    left = {"graph": (xl * NY + lax.rem(y + NY - 1, NY)) * NC + c}
    across = {"graph": ((1 - xl) * NY + y) * NC + c}

    def chip_peer(k):
        return lax.rem(chip + k, chips)

    def signal(sem, device):
        pl.semaphore_signal(sem, inc=1, device_id=device, device_id_type=MESH)

    def remote(src, dst, send, recv, device):
        return pltpu.make_async_remote_copy(
            src_ref=src,
            dst_ref=dst,
            send_sem=send,
            recv_sem=recv,
            device_id=device,
            device_id_type=MESH,
        )

    barrier = pltpu.get_barrier_semaphore()
    signal(barrier, sibling)

    @pl.loop(1, chips)
    def _(k):
        signal(barrier, {"graph": chip_peer(k) * NC + c})

    @pl.loop(1, n_dp)
    def _(k):
        signal(barrier, {"dp": lax.rem(dp + k, n_dp)})

    load_x = pltpu.make_async_copy(x_hbm, x_ref, load_sem.at[0])
    load_x.start()
    load_we = pltpu.make_async_copy(we_hbm, we_ref, load_sem.at[1])
    load_we.start()

    hrows = h_ref[...].astype(F32)
    own_rows = jnp.concatenate([hrows[:, :half], hrows[:, half:]], axis=0).astype(BF16)
    table[chip, c] = own_rows
    pl.semaphore_wait(barrier, chips + n_dp - 1)

    def table_copy(k):
        return remote(
            table.at[chip, c],
            table.at[chip, c],
            ag_send.at[k],
            ag_recv.at[chip],
            {"graph": chip_peer(k) * NC + c},
        )

    def table_arrival(k):
        s = chip_peer(k)
        return remote(
            table.at[s, c], table.at[s, c], ag_send.at[k], ag_recv.at[s], sibling
        )

    def forward(k):
        s = chip_peer(k)
        return remote(
            table.at[s, c], table.at[s, c], sib_send.at[s], sib_recv.at[s], sibling
        )

    def forward_arrival(k):
        s = chip_peer(k)
        return remote(
            table.at[s, oc], table.at[s, oc], sib_send.at[s], sib_recv.at[s], sibling
        )

    @pl.loop(1, chips)
    def _(k):
        table_copy(k).start()

    forward(0).start()

    edge_of_slot = lax.broadcasted_iota(jnp.int32, (edges, trips), 0)
    edge_base = g * edges
    atom_base = g * atoms_dev
    hits_out = (edge_of_slot == tout_ref[...] - edge_base).astype(F32).astype(BF16)
    target_hits = (
        (lax.broadcasted_iota(jnp.int32, (16, edges), 0) == tgt_ref[...] - atom_base)
        .astype(F32)
        .astype(BF16)
    )
    a_of = dot(target_hits, hits_out)
    slot = lax.broadcasted_iota(jnp.int32, (1, trips), 1)
    a_of = jnp.where(slot < counts_ref[0, 0] * BLOCK, a_of, 0.0)
    hits_in = (edge_of_slot == tin_ref[...] - edge_base).astype(F32).astype(BF16)
    basis = basis_ref[...].astype(F32)
    group = 256 // nb
    for q in range(atoms_dev // group):
        spreadout = jnp.concatenate(
            [basis * a_of[a : a + 1, :] for a in range(q * group, (q + 1) * group)], axis=0
        ).astype(BF16)
        mt_ref[:, q * 256 : (q + 1) * 256] = dot(hits_in, spreadout, NT).astype(BF16)
    cot = cot_ref[...].astype(F32)
    wb = wb_ref[...].astype(F32)
    for a in range(atoms_dev):
        g_ref[a * nb : (a + 1) * nb, :] = (wb * cot[a : a + 1, :]).astype(BF16)
    for j in range(width // 256):
        js = slice(j * 256, (j + 1) * 256)
        gm_ref[:, js] = dot(mt_ref[...], g_ref[:, js])

    @pl.loop(1, chips)
    def _(k):
        table_arrival(k).wait_recv()
        forward(k).start()

    @pl.loop(0, chips)
    def _(k):
        forward_arrival(k).wait_recv()

    packed = table[...].astype(F32).reshape(chips * NC, 2 * atoms_dev, half)
    tab[:, :half] = packed[:, :atoms_dev, :].reshape(chips * NC * atoms_dev, half).astype(BF16)
    tab[:, half:] = packed[:, atoms_dev:, :].reshape(chips * NC * atoms_dev, half).astype(BF16)

    atom_of_edge = lax.broadcasted_iota(jnp.int32, (tab.shape[0], edges), 0)
    hits = (
        (atom_of_edge == src_ref[...]).astype(F32) + (atom_of_edge == tgt_ref[...]).astype(F32)
    ).astype(BF16)
    load_x.wait()
    for j in range(width // 256):
        js = slice(j * 256, (j + 1) * 256)
        ends = dot(hits, tab[:, js], TN)
        joined_ref[:, js] = (x_ref[:, js].astype(F32) + ends).astype(BF16)
    load_we.wait()

    def owner_of(number):
        return (number // NC) % NY, number // (NC * NY), number % NC

    for j in range(width // 256):
        js = slice(j * 256, (j + 1) * 256)
        pre = dot(joined_ref[...], we_ref[:, js])
        logistic = 1.0 / (1.0 + jnp.exp(-pre))
        message = (pre * logistic).astype(BF16)
        slope = logistic * (1.0 + pre * (1.0 - logistic))
        gp_ref[:, js] = (gm_ref[:, js] * slope).astype(BF16)
        spread_sum = dot(mt_ref[...], message, TN)
        gwb = jnp.zeros((nb, 256), F32)
        for a in range(atoms_dev):
            gwb = gwb + spread_sum[a * nb : (a + 1) * nb, :] * cot[a : a + 1, js]
        both = jnp.concatenate([gwb, pltpu.roll(gwb, 256 - 16, 1)], axis=0)
        turned = both.T.astype(BF16).reshape(8, 2, 16, 128)
        for k in range(8):
            py, px, pc = owner_of(j * 8 + k)
            part[py, px, pc, :, wcols:bcols] = turned[k, 0]
    for i in range(width // 256):
        gw = dot(joined_ref[:, i * 256 : (i + 1) * 256], gp_ref[...], TN).astype(BF16)
        for k in range(8):
            py, px, pc = owner_of(i * 8 + k)
            part[py, px, pc, :, :width] = gw[k * 32 : k * 32 + 16]
            part[py, px, pc, :, width:wcols] = gw[k * 32 + 16 : k * 32 + 32]

    for j in range(width // 256):
        js = slice(j * 256, (j + 1) * 256)
        gx_ref[:, js] = dot(gp_ref[...], we_ref[js, :], NT).astype(BF16)
    store_gx = pltpu.make_async_copy(gx_ref, gx_hbm, load_sem.at[2])
    store_gx.start()
    lo = dot(hits, gx_ref[:, :half])
    hi = dot(hits, gx_ref[:, half:])
    for number in range(chips * NC):
        py, px, pc = owner_of(number)
        rows = slice(number * atoms_dev, (number + 1) * atoms_dev)
        part[py, px, pc, :, bcols:] = jnp.concatenate([lo[rows], hi[rows]], axis=0).astype(BF16)

    core_copies = []
    for i, away in enumerate(ORDER):
        there = lax.rem(y + away, NY)
        copy = remote(
            part.at[there, :, oc], from_core.at[i], core_send.at[i], core_recv.at[i], sibling
        )
        copy.start()
        core_copies.append(copy)

    def add_core(i):
        core_copies[i].wait_recv()
        there = lax.rem(y + ORDER[i], NY)
        for px in range(NX):
            part[there, px, c] = (
                part[there, px, c].astype(F32) + from_core[i, px].astype(F32)
            ).astype(BF16)

    to_right, to_left = [], []
    for k, (dist, side) in enumerate(zip(DIST, HALF)):
        if k == 0:
            add_core(0)
        elif k % 2:
            add_core(k)
            add_core(k + 1)
        there = lax.rem(y + dist, NY)
        if k >= 2:
            to_right[k - 2].wait_recv()
            part[there, side, c] = (
                part[there, side, c].astype(F32) + from_left[k - 2].astype(F32)
            ).astype(BF16)
        copy = remote(
            part.at[there, side, c],
            from_left.at[k],
            right_send.at[k],
            right_recv.at[k],
            right,
        )
        copy.start()
        to_right.append(copy)
        there = lax.rem(y + NY - dist, NY)
        if k >= 2:
            to_left[k - 2].wait_recv()
            part[there, 1 - side, c] = (
                part[there, 1 - side, c].astype(F32) + from_right[k - 2].astype(F32)
            ).astype(BF16)
        copy = remote(
            part.at[there, 1 - side, c],
            from_right.at[k],
            left_send.at[k],
            left_recv.at[k],
            left,
        )
        copy.start()
        to_left.append(copy)
    core_copies[7].wait_recv()
    for k in (5, 6):
        to_right[k].wait_recv()
        to_left[k].wait_recv()
    last = len(DIST) - 1
    for px in range(NX):
        acc[px] = (
            part[y, px, c].astype(F32)
            + from_core[7, px].astype(F32)
            + from_left[last - px].astype(F32)
            + from_right[last - 1 + px].astype(F32)
        )

    x_out[...] = acc[1 - xl].astype(BF16)
    pair = remote(x_out, x_in, pair_send, pair_recv, across)
    pair.start()
    pair.wait_recv()
    total = acc[xl] + x_in[...].astype(F32)

    for b in range(blocks):
        dp_out[b] = total[:, b * 128 : (b + 1) * 128].astype(BF16)

    def share(d):
        return remote(
            dp_out.at[d], dp_in.at[dp], dps_send.at[d], dps_recv.at[dp], {"dp": d}
        )

    def share_arrival(s):
        return remote(
            dp_out.at[0], dp_in.at[s], dps_send.at[0], dps_recv.at[s], {"dp": s}
        )

    @pl.loop(0, blocks)
    def _(d):
        @pl.when(d != dp)
        def _():
            share(d).start()

    grad_h = total[:, bcols:]
    gh_ref[...] = (
        cot + jnp.concatenate([grad_h[:atoms_dev], grad_h[atoms_dev:]], axis=1)
    ).astype(BF16)

    def spread_total(k):
        d = lax.rem(dp + k, n_dp)
        return remote(
            dp_all.at[dp], dp_all.at[dp], dpg_send.at[k], dpg_recv.at[dp], {"dp": d}
        )

    @pl.when(dp < blocks)
    def _():
        dp_in[dp] = dp_out[dp]

        @pl.loop(1, n_dp)
        def _(k):
            share_arrival(lax.rem(dp + k, n_dp)).wait_recv()

        dp_all[dp] = jnp.sum(dp_in[...].astype(F32), axis=0)

        @pl.loop(1, n_dp)
        def _(k):
            spread_total(k).start()

    @pl.loop(0, blocks)
    def _(s):
        @pl.when(s != dp)
        def _():
            remote(
                dp_all.at[s], dp_all.at[s], dpg_send.at[0], dpg_recv.at[s], {"dp": s}
            ).wait_recv()

    per_row = width // 128
    for b in range(blocks - 1):
        r, q = b // per_row, b % per_row
        gw_ref[r * 16 : (r + 1) * 16, q * 128 : (q + 1) * 128] = dp_all[b]
    gwb_ref[...] = dp_all[blocks - 1]

    @pl.when(dp < blocks)
    def _():
        @pl.loop(1, n_dp)
        def _(k):
            spread_total(k).wait_send()

    @pl.loop(0, blocks)
    def _(d):
        @pl.when(d != dp)
        def _():
            share(d).wait_send()

    pair.wait_send()
    for copy in core_copies + to_right + to_left:
        copy.wait_send()

    @pl.loop(1, chips)
    def _(k):
        table_copy(k).wait_send()

    @pl.loop(0, chips)
    def _(k):
        forward(k).wait_send()

    store_gx.wait()


def shards(
    atom_h,
    edge_x,
    edge_source,
    edge_target,
    trip_in,
    trip_out,
    basis,
    block_counts,
    atom_cotangent,
    weight_edge,
    weight_basis,
):
    n_dp = lax.axis_size("dp")
    edges, width = edge_x.shape[1:]
    nb, trips = basis.shape[1:]
    atoms_dev = atom_h.shape[1]
    chips = NX * NY
    half = width // 2
    cols = 2 * width + 128 + half
    blocks = (2 * width + 128) // 128
    steps = len(DIST)
    vmem = pl.BlockSpec(memory_space=pltpu.VMEM)
    hbm = pl.BlockSpec(memory_space=pl.ANY)
    smem = pl.BlockSpec(memory_space=pltpu.SMEM)
    dma = pltpu.SemaphoreType.DMA
    grad_x, grad_h, grad_w, grad_wb = pl.pallas_call(
        lambda *refs: kernel(n_dp, *refs),
        out_shape=(
            jax.ShapeDtypeStruct((edges, width), BF16),
            jax.ShapeDtypeStruct((atoms_dev, width), BF16),
            jax.ShapeDtypeStruct((width // (chips * NC), width), F32),
            jax.ShapeDtypeStruct((16, 128), F32),
        ),
        in_specs=[vmem, hbm, vmem, vmem, vmem, vmem, vmem, smem, vmem, hbm, vmem],
        out_specs=(hbm, vmem, vmem, vmem),
        scratch_shapes=[
            pltpu.VMEM((edges, width), BF16),
            pltpu.VMEM((width, width), BF16),
            pltpu.VMEM((chips, NC, 2 * atoms_dev, half), BF16),
            pltpu.VMEM((chips * NC * atoms_dev, width), BF16),
            pltpu.VMEM((edges, atoms_dev * nb), BF16),
            pltpu.VMEM((atoms_dev * nb, width), BF16),
            pltpu.VMEM((edges, width), F32),
            pltpu.VMEM((edges, width), BF16),
            pltpu.VMEM((edges, width), BF16),
            pltpu.VMEM((edges, width), BF16),
            pltpu.VMEM((NY, NX, NC, 16, cols), BF16),
            pltpu.VMEM((NY, NX, 16, cols), BF16),
            pltpu.VMEM((steps, 16, cols), BF16),
            pltpu.VMEM((steps, 16, cols), BF16),
            pltpu.VMEM((NX, 16, cols), F32),
            pltpu.VMEM((16, cols), BF16),
            pltpu.VMEM((16, cols), BF16),
            pltpu.VMEM((blocks, 16, 128), BF16),
            pltpu.VMEM((n_dp, 16, 128), BF16),
            pltpu.VMEM((blocks, 16, 128), F32),
            dma((3,)),
            dma((chips,)),
            dma((chips,)),
            dma((chips,)),
            dma((chips,)),
            dma((NY,)),
            dma((NY,)),
            dma((steps,)),
            dma((steps,)),
            dma((steps,)),
            dma((steps,)),
            dma,
            dma,
            dma((blocks,)),
            dma((n_dp,)),
            dma((n_dp,)),
            dma((n_dp,)),
        ],
        compiler_params=pltpu.CompilerParams(
            collective_id=0, has_side_effects=True, vmem_limit_bytes=48 * 1024 * 1024
        ),
    )(
        atom_h[0],
        edge_x[0],
        edge_source,
        edge_target,
        trip_in,
        trip_out,
        basis[0],
        block_counts,
        atom_cotangent[0],
        weight_edge,
        weight_basis,
    )
    turned = grad_wb.T
    grad_wb = jnp.concatenate([turned[:nb], turned[nb:]], axis=1)
    return (grad_x[None], grad_h[None], grad_w, grad_wb)


def solution(mesh):
    placed = (
        P("dp", "graph", None),
        P("dp", "graph", None),
        P("dp", "graph"),
        P("dp", "graph"),
        P("dp", "graph"),
        P("dp", "graph"),
        P("dp", None, "graph"),
        P("dp", "graph"),
        P("dp", "graph", None),
        P(),
        P(),
    )
    return jax.shard_map(
        shards,
        mesh=mesh,
        in_specs=placed,
        out_specs=(
            P("dp", "graph", None),
            P("dp", "graph", None),
            P("graph", None),
            P(None, "graph"),
        ),
        check_vma=False,
    )
```

time: 772 us -> 89.5 us (0.12)
  the two profiles are of different devices: /device:TPU:6 before, /device:TPU:2 now
where the time goes in v1:
time: 89.5 us; the launch traced here: 89.1 us
  Pallas kernels  76.1 us (85%)
  local copies, waits for them, and re-layouts  11.1 us (12%)
  between operations  1.31 us (1%)
    pallas_call x1, Pallas kernels, shards(): pl.pallas_call(lambda *refs: kernel(n_dp, *refs), out_shape=(jax.ShapeDty...  76.1 us
    unnamed x23, local copies, waits for them, and re-layouts  11 us

profile of v1, /device:TPU:2, one launch (start us, length us, event | category | flops | bytes accessed | tf_op | source)
XLA Modules:
  0.0 89.1 jit_solution(6414997899643237552)
XLA Ops:
  1.3 0.0 copy-start
  1.3 1.6 %copy-done = bf16[1024,1024]{1,0:T(8,128)(2,1)S(1)} copy-done((bf16[1024,1024]{1,0:T(8,128)(2,1)S(1)}, bf16[1024,1024]{1,0:T(8,128)(2,1)}, u32[]{:S(2)}) %copy-start) | copy-done | bytes 2097176
  2.9 0.0 copy-start.1
  2.9 1.2 %copy-done.1 = bf16[1,512,1024]{2,1,0:T(8,128)(2,1)S(1)} copy-done((bf16[1,512,1024]{2,1,0:T(8,128)(2,1)S(1)}, bf16[1,512,1024]{2,1,0:T(8,128)(2,1)}, u32[]{:S(2)}) %copy-start.1) | copy-done | bytes 1048600
  4.1 0.0 copy-start.2
  4.1 0.9 %copy-done.2 = bf16[1,64,1024]{2,1,0:T(8,128)(2,1)S(1)} copy-done((bf16[1,64,1024]{2,1,0:T(8,128)(2,1)S(1)}, bf16[1,64,1024]{2,1,0:T(8,128)(2,1)}, u32[]{:S(2)}) %copy-start.2) | copy-done | bytes 131096
  5.0 0.0 copy-start.3
  5.0 0.9 %copy-done.3 = bf16[64,1024]{1,0:T(8,128)(2,1)S(1)} copy-done((bf16[64,1024]{1,0:T(8,128)(2,1)S(1)}, bf16[64,1024]{1,0:T(8,128)(2,1)}, u32[]{:S(2)}) %copy-start.3) | copy-done | bytes 131096
  5.9 0.0 copy-start.4
  5.9 0.7 copy-done.4
  6.6 0.0 copy-start.5
  6.6 0.7 copy-done.5
  7.3 0.0 copy-start.6
  7.3 0.7 copy-done.6
  8.0 0.0 copy-start.7
  8.0 0.7 copy-done.7
  8.7 0.0 copy-start.8
  8.7 0.7 copy-done.8
  9.4 0.0 copy-start.9
  9.4 0.7 copy-done.9
  10.1 76.1 %shard_map.138 = (bf16[512,1024]{1,0:T(8,128)(2,1)S(1)}, bf16[8,1024]{1,0:T(8,128)(2,1)S(1)}, f32[32,1024]{1,0:T(8,128)S(1)}, f32[16,128]{1,0:T(8,128)S(1)}) custom-call(bf16[8,1024]{1,0:T(8,128)(2,1)S(1)} %bitcast.11, bf16[512,1024]{1,0:T(8,128)(2,1)S(1)} %bitcast.7, s32[1,512]{1,0:T(1,128)S(1)} %copy-done.8, s32[1,512]{1,0:T(1,128)S(1)} %copy-done.9, ...), custom_call_target="tpu_custom_call" | custom-call | tf_op jit(solution)/shard_map/pallas_call | solution.py:446
  86.2 0.1 fusion
  86.2 0.6 pad_maximum_fusion
  86.8 1.0 %copy.19 = bf16[1,512,1024]{2,1,0:T(8,128)(2,1)} copy(bf16[1,512,1024]{2,1,0:T(8,128)(2,1)S(1)} %bitcast.8) | data formatting | bytes 2097152
  87.8 0.6 copy.20
  88.4 0.7 copy.21
Async XLA Ops:
  1.3 1.6 %copy-start = (bf16[1024,1024]{1,0:T(8,128)(2,1)S(1)}, bf16[1024,1024]{1,0:T(8,128)(2,1)}, u32[]{:S(2)}) copy-start(bf16[1024,1024]{1,0:T(8,128)(2,1)} %refs_9_.1) | copy-start | bytes 6291460
  2.9 1.2 %copy-start.1 = (bf16[1,512,1024]{2,1,0:T(8,128)(2,1)S(1)}, bf16[1,512,1024]{2,1,0:T(8,128)(2,1)}, u32[]{:S(2)}) copy-start(bf16[1,512,1024]{2,1,0:T(8,128)(2,1)} %param.12) | copy-start | bytes 3145732
  4.1 0.9 %copy-start.2 = (bf16[1,64,1024]{2,1,0:T(8,128)(2,1)S(1)}, bf16[1,64,1024]{2,1,0:T(8,128)(2,1)}, u32[]{:S(2)}) copy-start(bf16[1,64,1024]{2,1,0:T(8,128)(2,1)} %param.17) | copy-start | bytes 393220
  5.0 0.9 %copy-start.3 = (bf16[64,1024]{1,0:T(8,128)(2,1)S(1)}, bf16[64,1024]{1,0:T(8,128)(2,1)}, u32[]{:S(2)}) copy-start(bf16[64,1024]{1,0:T(8,128)(2,1)} %refs_10_.1) | copy-start | bytes 393220
  5.9 0.7 copy-start.4
  6.6 0.7 copy-start.5
  7.3 0.7 copy-start.6
  8.0 0.7 copy-start.7
  8.7 0.7 copy-start.8
  9.4 0.7 copy-start.9

commit v2 on v1

v2 whole, which is shorter than its diff:
```python
import jax
import jax.numpy as jnp
from jax import lax
from jax.experimental import pallas as pl
from jax.experimental.pallas import tpu as pltpu
from jax.sharding import PartitionSpec as P

BLOCK = 128
NX, NY, NC = 2, 8, 2
MESH = pl.DeviceIdType.MESH
F32 = jnp.float32
BF16 = jnp.bfloat16
TN = (((0,), (0,)), ((), ()))
NT = (((1,), (1,)), ((), ()))
DIST = (4, 3, 3, 2, 2, 1, 1)
HALF = (0, 1, 0, 1, 0, 1, 0)
PLACES = (0, -1, -2, 1, 2, -3, 3, 4)


def dot(a, b, dims=None):
    if dims is None:
        return jnp.dot(a, b, preferred_element_type=F32)
    return lax.dot_general(a, b, dims, preferred_element_type=F32)


def kernel(
    n_dp,
    h_hbm,
    x_hbm,
    src_hbm,
    tgt_hbm,
    tin_hbm,
    tout_hbm,
    basis_hbm,
    counts_hbm,
    cot_hbm,
    we_hbm,
    wb_hbm,
    gx_hbm,
    gh_ref,
    gw_ref,
    gwb_ref,
    h_ref,
    x_ref,
    src_ref,
    tgt_ref,
    tin_ref,
    tout_ref,
    basis_ref,
    counts_ref,
    cot_ref,
    we_ref,
    wb_ref,
    table,
    tab,
    mt_ref,
    g_ref,
    gm_ref,
    joined_ref,
    gp_ref,
    gx_ref,
    msg_ref,
    part_w,
    part_s,
    core_w,
    core_s,
    left_w,
    left_s,
    right_w,
    right_s,
    acc_w,
    acc_s,
    x_out_w,
    x_in_w,
    x_out_b,
    x_in_b,
    x_out_h,
    x_in_h,
    dp_out,
    dp_in,
    dp_all,
    load_sem,
    tab_send,
    tab_recv,
    tabx_send,
    tabx_recv,
    sib_send,
    sib_recv,
    core_send,
    core_recv,
    left_send,
    left_recv,
    right_send,
    right_recv,
    x_send,
    x_recv,
    dps_send,
    dps_recv,
    dpg_send,
    dpg_recv,
):
    edges, width = x_ref.shape
    nb, trips = basis_ref.shape
    atoms_dev = h_ref.shape[0]
    half = width // 2
    tiles = width // 128
    nz = n_dp // 2
    dp = lax.axis_index("dp")
    g = lax.axis_index("graph")
    chip = lax.div(g, NC)
    c = lax.rem(g, NC)
    xl = lax.div(chip, NY)
    y = lax.rem(chip, NY)
    oc = 1 - c
    xh = lax.div(dp, nz)
    z = lax.rem(dp, nz)

    def along(offset):
        return lax.rem(y + (offset + NY), NY)

    def y_peer(offset):
        return {"graph": (xl * NY + along(offset)) * NC + c}

    sibling = {"graph": chip * NC + oc}
    right, left = y_peer(1), y_peer(-1)
    other_graph = ((1 - xl) * NY + y) * NC + c
    other_dp = (1 - xh) * nz + z
    across = {"graph": other_graph}
    x_peers = (across, {"dp": other_dp}, {"dp": other_dp, "graph": other_graph})

    def signal(sem, device):
        pl.semaphore_signal(sem, inc=1, device_id=device, device_id_type=MESH)

    def remote(src, dst, send, recv, device):
        return pltpu.make_async_remote_copy(
            src_ref=src,
            dst_ref=dst,
            send_sem=send,
            recv_sem=recv,
            device_id=device,
            device_id_type=MESH,
        )

    sent = []

    def begin(copy):
        copy.start()
        sent.append(copy)

    loads = [
        pltpu.make_async_copy(src, dst, load_sem.at[i])
        for i, (src, dst) in enumerate(
            [
                (h_hbm, h_ref),
                (tout_hbm, tout_ref),
                (tgt_hbm, tgt_ref),
                (tin_hbm, tin_ref),
                (counts_hbm, counts_ref),
                (basis_hbm, basis_ref),
                (wb_hbm, wb_ref),
                (cot_hbm, cot_ref),
                (src_hbm, src_ref),
                (x_hbm, x_ref),
                (we_hbm, we_ref),
            ]
        )
    ]
    for load in loads:
        load.start()
    load_h, load_x, load_we = loads[0], loads[-2], loads[-1]

    barrier = pltpu.get_barrier_semaphore()
    greeted = [sibling, right, left, y_peer(2), y_peer(-2), across, x_peers[2]]
    for peer in greeted:
        signal(barrier, peer)

    @pl.loop(1, n_dp)
    def _(k):
        signal(barrier, {"dp": lax.rem(dp + k, n_dp)})

    load_h.wait()
    hrows = h_ref[...].astype(F32)
    own_rows = jnp.concatenate([hrows[:, :half], hrows[:, half:]], axis=0).astype(BF16)
    table[xl, y, c] = own_rows
    pl.semaphore_wait(barrier, len(greeted) + n_dp - 1)

    def block(offset, part=None):
        if part is None:
            return table.at[xl, along(offset), c]
        return table.at[xl, along(offset), c, :, part * (half // 2) : (part + 1) * (half // 2)]

    number = {-1: 0, -2: 1, 1: 2, 2: 3, -3: 4, 3: 5, -4: 6, 4: 7}
    side = {-4: 0, 4: 1}

    def table_send(offset, to):
        seen = offset - to
        i, ref = number[seen], block(offset, side.get(seen))
        begin(remote(ref, ref, tab_send.at[i], tab_recv.at[i], y_peer(to)))

    def table_wait(seen):
        i, ref = number[seen], block(seen, side.get(seen))
        remote(ref, ref, tab_send.at[i], tab_recv.at[i], sibling).wait_recv()

    def across_send(i):
        ref = block(PLACES[i])
        begin(remote(ref, ref, tabx_send.at[i], tabx_recv.at[i], across))

    def across_wait(i):
        ref = table.at[1 - xl, along(PLACES[i]), c]
        remote(ref, ref, tabx_send.at[i], tabx_recv.at[i], sibling).wait_recv()

    def sibling_send(i, other):
        ref = table.at[(1 - xl) if other else xl, along(PLACES[i]), c]
        j = other * NY + i
        begin(remote(ref, ref, sib_send.at[j], sib_recv.at[j], sibling))

    def sibling_wait(i, other):
        ref = table.at[(1 - xl) if other else xl, along(PLACES[i]), oc]
        j = other * NY + i
        remote(ref, ref, sib_send.at[j], sib_recv.at[j], sibling).wait_recv()

    for to in (2, -2, 1, -1):
        table_send(0, to)
    across_send(0)
    sibling_send(0, 0)

    for load in loads[1:-2]:
        load.wait()
    edge_of_slot = lax.broadcasted_iota(jnp.int32, (edges, trips), 0)
    edge_base = g * edges
    atom_base = g * atoms_dev
    hits_out = (edge_of_slot == tout_ref[...] - edge_base).astype(F32).astype(BF16)
    target_hits = (
        (lax.broadcasted_iota(jnp.int32, (16, edges), 0) == tgt_ref[...] - atom_base)
        .astype(F32)
        .astype(BF16)
    )
    a_of = dot(target_hits, hits_out)
    slot = lax.broadcasted_iota(jnp.int32, (1, trips), 1)
    a_of = jnp.where(slot < counts_ref[0, 0] * BLOCK, a_of, 0.0)

    for seen, to in ((-2, 1), (2, -1), (-2, 2), (2, -2)):
        if abs(to) == 1:
            table_wait(seen)
        table_send(seen, to)
    table_wait(-1)
    table_wait(1)
    for i in (2, 4, 1, 3):
        across_send(i)
    for i in (2, 4, 1, 3):
        sibling_send(i, 0)

    hits_in = (edge_of_slot == tin_ref[...] - edge_base).astype(F32).astype(BF16)
    basis = basis_ref[...].astype(F32)
    group = 256 // nb
    for q in range(atoms_dev // group):
        spreadout = jnp.concatenate(
            [basis * a_of[a : a + 1, :] for a in range(q * group, (q + 1) * group)], axis=0
        ).astype(BF16)
        mt_ref[:, q * 256 : (q + 1) * 256] = dot(hits_in, spreadout, NT).astype(BF16)

    for seen in (-3, 3, -4, 4):
        table_wait(seen)
    for i in (5, 6, 7):
        across_send(i)
    for i in (5, 6, 7):
        sibling_send(i, 0)
    for i in (0, 2, 4, 1, 3):
        across_wait(i)
        sibling_send(i, 1)

    cot = cot_ref[...].astype(F32)
    wb = wb_ref[...].astype(F32)
    for a in range(atoms_dev):
        g_ref[a * nb : (a + 1) * nb, :] = (wb * cot[a : a + 1, :]).astype(BF16)
    for j in range(width // 256):
        js = slice(j * 256, (j + 1) * 256)
        gm_ref[:, js] = dot(mt_ref[...], g_ref[:, js])

    for i in (5, 6, 7):
        across_wait(i)
        sibling_send(i, 1)
    for i in range(NY):
        sibling_wait(i, 0)
        sibling_wait(i, 1)

    all_atoms = NX * NY * NC * atoms_dev
    packed = table[...].astype(F32).reshape(NX * NY * NC, 2 * atoms_dev, half)
    tab[:, :half] = packed[:, :atoms_dev, :].reshape(all_atoms, half).astype(BF16)
    tab[:, half:] = packed[:, atoms_dev:, :].reshape(all_atoms, half).astype(BF16)

    atom_of_edge = lax.broadcasted_iota(jnp.int32, (all_atoms, edges), 0)
    hits = (
        (atom_of_edge == src_ref[...]).astype(F32) + (atom_of_edge == tgt_ref[...]).astype(F32)
    ).astype(BF16)
    load_x.wait()
    for j in range(width // 256):
        js = slice(j * 256, (j + 1) * 256)
        ends = dot(hits, tab[:, js], TN)
        joined_ref[:, js] = (x_ref[:, js].astype(F32) + ends).astype(BF16)
    load_we.wait()
    for j in range(width // 256):
        js = slice(j * 256, (j + 1) * 256)
        pre = dot(joined_ref[...], we_ref[:, js])
        logistic = 1.0 / (1.0 + jnp.exp(-pre))
        msg_ref[:, js] = (pre * logistic).astype(BF16)
        slope = logistic * (1.0 + pre * (1.0 - logistic))
        gp_ref[:, js] = (gm_ref[:, js] * slope).astype(BF16)

    def core_copy(part, landing, sem, there):
        return remote(
            part.at[there, :, oc],
            landing.at[there],
            core_send.at[sem, there],
            core_recv.at[sem, there],
            sibling,
        )

    near = lax.div(y, 4)
    for far in (1 - near, near):
        for px in range(NX):
            rows = pl.ds(pl.multiple_of((px * 2 + far) * 256, 256), 256)
            gw = dot(joined_ref[:, rows], gp_ref[...], TN).astype(BF16)
            for k in range(8):
                py = far * 4 + k // 2
                part_w[py, px, k % 2, :, :width] = gw[k * 32 : k * 32 + 16]
                part_w[py, px, k % 2, :, width:] = gw[k * 32 + 16 : k * 32 + 32]
        for m in range(4):
            begin(core_copy(part_w, core_w, 0, far * 4 + lax.rem(y + m, 4)))

    def stream(sem, part, landing, from_left, from_right):
        def add_core(offset):
            there = along(offset)
            core_copy(part, landing, sem, there).wait_recv()
            for px in range(NX):
                part[there, px, c] = (
                    part[there, px, c].astype(F32) + landing[there, px].astype(F32)
                ).astype(BF16)

        def copies(k):
            right_ref = part.at[along(DIST[k]), HALF[k], c]
            left_ref = part.at[along(-DIST[k]), 1 - HALF[k], c]
            return (
                remote(
                    right_ref, from_left.at[k], right_send.at[sem, k], right_recv.at[sem, k], right
                ),
                remote(
                    left_ref, from_right.at[k], left_send.at[sem, k], left_recv.at[sem, k], left
                ),
            )

        def step(k):
            if k == 0:
                add_core(4)
            elif k % 2:
                add_core(DIST[k])
                add_core(-DIST[k])
            to_right, to_left = copies(k)
            if k >= 2:
                before_right, before_left = copies(k - 2)
                there = along(DIST[k])
                before_right.wait_recv()
                part[there, HALF[k], c] = (
                    part[there, HALF[k], c].astype(F32) + from_left[k - 2].astype(F32)
                ).astype(BF16)
                begin(to_right)
                there = along(-DIST[k])
                before_left.wait_recv()
                part[there, 1 - HALF[k], c] = (
                    part[there, 1 - HALF[k], c].astype(F32) + from_right[k - 2].astype(F32)
                ).astype(BF16)
                begin(to_left)
            else:
                begin(to_right)
                begin(to_left)

        def finish():
            core_copy(part, landing, sem, y).wait_recv()
            for k in (5, 6):
                for copy in copies(k):
                    copy.wait_recv()
            return [
                part[y, px, c].astype(F32)
                + landing[y, px].astype(F32)
                + from_left[6 - px].astype(F32)
                + from_right[5 + px].astype(F32)
                for px in range(NX)
            ]

        return step, finish

    step_w, finish_w = stream(0, part_w, core_w, left_w, right_w)
    step_s, finish_s = stream(1, part_s, core_s, left_s, right_s)

    def owner_of(number):
        return (number // NC) % NY, number // (NC * NY), number % NC

    def basis_piece(j):
        js = slice(j * 256, (j + 1) * 256)
        spread_sum = dot(mt_ref[...], msg_ref[:, js], TN)
        gwb = jnp.zeros((nb, 256), F32)
        for a in range(atoms_dev):
            gwb = gwb + spread_sum[a * nb : (a + 1) * nb, :] * cot[a : a + 1, js]
        both = jnp.concatenate([gwb, pltpu.roll(gwb, 256 - 16, 1)], axis=0)
        turned = both.T.astype(BF16).reshape(8, 2, 16, 128)
        for k in range(8):
            py, px, pc = owner_of(j * 8 + k)
            part_s[py, px, pc, :, :128] = turned[k, 0]

    def grad_x_piece(j):
        js = slice(j * 256, (j + 1) * 256)
        gx_ref[:, js] = dot(gp_ref[...], we_ref[js, :], NT).astype(BF16)

    def atoms_piece():
        lo = dot(hits, gx_ref[:, :half])
        hi = dot(hits, gx_ref[:, half:])
        for number in range(NX * NY * NC):
            py, px, pc = owner_of(number)
            rows = slice(number * atoms_dev, (number + 1) * atoms_dev)
            part_s[py, px, pc, :, 128:] = jnp.concatenate([lo[rows], hi[rows]], axis=0).astype(
                BF16
            )

    step_w(0)
    step_w(1)
    grad_x_piece(0)
    grad_x_piece(1)
    step_w(2)
    grad_x_piece(2)
    grad_x_piece(3)
    step_w(3)
    store_gx = pltpu.make_async_copy(gx_ref, gx_hbm, load_sem.at[11])
    store_gx.start()
    basis_piece(0)
    basis_piece(1)
    step_w(4)
    basis_piece(2)
    basis_piece(3)
    step_w(5)
    atoms_piece()
    for m in (4, 3, 5, 2, 6, 1, 7, 0):
        begin(core_copy(part_s, core_s, 1, along(m - NY)))
    step_w(6)
    step_s(0)
    step_s(1)

    for px, value in enumerate(finish_w()):
        acc_w[px, 0] = value[:, :width]
        acc_w[px, 1] = value[:, width:]
    quarters = ((1 - xl, xh), (xl, 1 - xh), (1 - xl, 1 - xh))

    def x_copy(kind, p, out, landing):
        return remote(out, landing, x_send.at[kind, p], x_recv.at[kind, p], x_peers[p])

    def x_copy_w(p):
        return x_copy(0, p, x_out_w.at[p], x_in_w.at[p])

    def x_copy_b(p):
        return x_copy(1, p, x_out_b.at[p], x_in_b.at[p])

    x_copy_h = x_copy(2, 0, x_out_h, x_in_h)
    for p, (qx, qh) in enumerate(quarters):
        x_out_w[p] = acc_w[qx, qh].astype(BF16)
        begin(x_copy_w(p))
    for k in range(2, len(DIST)):
        step_s(k)
    for px, value in enumerate(finish_s()):
        acc_s[px] = value
    for p, (qx, qh) in enumerate(quarters):
        x_out_b[p] = acc_s[qx, :, :128].astype(BF16)
        begin(x_copy_b(p))
    x_out_h[...] = acc_s[1 - xl, :, 128:].astype(BF16)
    begin(x_copy_h)

    total_w = acc_w[xl, xh]
    total_b = acc_s[xl, :, :128]
    for p in range(3):
        x_copy_w(p).wait_recv()
        total_w = total_w + x_in_w[p].astype(F32)
    for p in range(3):
        x_copy_b(p).wait_recv()
        total_b = total_b + x_in_b[p].astype(F32)

    for t in range(tiles):
        dp_out[t] = total_w[:, t * 128 : (t + 1) * 128].astype(BF16)
    dp_out[tiles] = total_b.astype(BF16)
    mine = tiles + xh

    def share(t):
        return remote(
            dp_out.at[t], dp_in.at[z], dps_send.at[t], dps_recv.at[z], {"dp": xh * nz + t}
        )

    @pl.loop(0, mine)
    def _(t):
        @pl.when(t != z)
        def _():
            share(t).start()

    x_copy_h.wait_recv()
    grad_h = acc_s[xl, :, 128:] + x_in_h[...].astype(F32)
    gh_ref[...] = (
        cot + jnp.concatenate([grad_h[:atoms_dev], grad_h[atoms_dev:]], axis=1)
    ).astype(BF16)

    own_tile = xh * tiles + z

    def spread_total(k):
        return remote(
            dp_all.at[own_tile],
            dp_all.at[own_tile],
            dpg_send.at[k],
            dpg_recv.at[own_tile],
            {"dp": lax.rem(dp + k, n_dp)},
        )

    @pl.when(z < mine)
    def _():
        dp_in[z] = dp_out[z]

        @pl.loop(1, nz)
        def _(k):
            s = lax.rem(z + k, nz)
            remote(
                dp_out.at[0], dp_in.at[s], dps_send.at[0], dps_recv.at[s], sibling
            ).wait_recv()

        dp_all[own_tile] = jnp.sum(dp_in[...].astype(F32), axis=0).astype(BF16)

        @pl.loop(1, n_dp)
        def _(k):
            spread_total(k).start()

    @pl.loop(0, 2 * tiles + 1)
    def _(t):
        @pl.when(jnp.logical_or(t != own_tile, z >= mine))
        def _():
            remote(
                dp_all.at[t], dp_all.at[t], dpg_send.at[0], dpg_recv.at[t], sibling
            ).wait_recv()

    for t in range(2 * tiles):
        r, q = t // tiles, t % tiles
        gw_ref[r * 16 : (r + 1) * 16, q * 128 : (q + 1) * 128] = dp_all[t].astype(F32)
    gwb_ref[...] = dp_all[2 * tiles].astype(F32)

    @pl.when(z < mine)
    def _():
        @pl.loop(1, n_dp)
        def _(k):
            spread_total(k).wait_send()

    @pl.loop(0, mine)
    def _(t):
        @pl.when(t != z)
        def _():
            share(t).wait_send()

    for copy in sent:
        copy.wait_send()
    store_gx.wait()


def write_out(gx, gh, gw, gwb, gx_hbm, gh_hbm, gw_hbm, gwb_hbm, gx_ref, gh_ref, gw_ref, in_ref, out_ref, get, put):
    rows = gx_ref.shape[0] // 4
    nb = out_ref.shape[1]
    moves = [(gwb, in_ref, out_ref, gwb_hbm), (gh, gh_ref, gh_ref, gh_hbm), (gw, gw_ref, gw_ref, gw_hbm)]
    for i in range(4):
        part = pl.ds(i * rows, rows)
        moves.append((gx.at[part], gx_ref.at[part], gx_ref.at[part], gx_hbm.at[part]))
    gets = [pltpu.make_async_copy(a, b, get.at[i]) for i, (a, b, _, _) in enumerate(moves)]
    puts = [pltpu.make_async_copy(a, b, put.at[i]) for i, (_, _, a, b) in enumerate(moves)]
    for copy in gets:
        copy.start()
    for i, copy in enumerate(puts):
        gets[i].wait()
        if i == 0:
            out_ref[:16, :] = in_ref[:, :nb]
            out_ref[16:, :] = in_ref[:, nb:]
        copy.start()
    for copy in puts:
        copy.wait()


def shards(
    atom_h,
    edge_x,
    edge_source,
    edge_target,
    trip_in,
    trip_out,
    basis,
    block_counts,
    atom_cotangent,
    weight_edge,
    weight_basis,
):
    n_dp = lax.axis_size("dp")
    edges, width = edge_x.shape[1:]
    nb, trips = basis.shape[1:]
    atoms_dev = atom_h.shape[1]
    owned = width // (NX * NY * NC)
    half = width // 2
    small = 128 + half
    steps = len(DIST)
    tiles = width // 128
    vmem = pl.BlockSpec(memory_space=pltpu.VMEM)
    hbm = pl.BlockSpec(memory_space=pltpu.HBM)
    dma = pltpu.SemaphoreType.DMA
    grad_x, grad_h, grad_w, grad_wb = pl.pallas_call(
        lambda *refs: kernel(n_dp, *refs),
        out_shape=(
            jax.ShapeDtypeStruct((edges, width), BF16),
            jax.ShapeDtypeStruct((atoms_dev, width), BF16),
            jax.ShapeDtypeStruct((owned, width), F32),
            jax.ShapeDtypeStruct((16, 128), F32),
        ),
        in_specs=[hbm] * 11,
        out_specs=(hbm, vmem, vmem, vmem),
        scratch_shapes=[
            pltpu.VMEM((atoms_dev, width), BF16),
            pltpu.VMEM((edges, width), BF16),
            pltpu.VMEM((1, edges), jnp.int32),
            pltpu.VMEM((1, edges), jnp.int32),
            pltpu.VMEM((1, trips), jnp.int32),
            pltpu.VMEM((1, trips), jnp.int32),
            pltpu.VMEM((nb, trips), BF16),
            pltpu.SMEM((1, 1), jnp.int32),
            pltpu.VMEM((atoms_dev, width), BF16),
            pltpu.VMEM((width, width), BF16),
            pltpu.VMEM((nb, width), BF16),
            pltpu.VMEM((NX, NY, NC, 2 * atoms_dev, half), BF16),
            pltpu.VMEM((NX * NY * NC * atoms_dev, width), BF16),
            pltpu.VMEM((edges, atoms_dev * nb), BF16),
            pltpu.VMEM((atoms_dev * nb, width), BF16),
            pltpu.VMEM((edges, width), F32),
            pltpu.VMEM((edges, width), BF16),
            pltpu.VMEM((edges, width), BF16),
            pltpu.VMEM((edges, width), BF16),
            pltpu.VMEM((edges, width), BF16),
            pltpu.VMEM((NY, NX, NC, 16, 2 * width), BF16),
            pltpu.VMEM((NY, NX, NC, 16, small), BF16),
            pltpu.VMEM((NY, NX, 16, 2 * width), BF16),
            pltpu.VMEM((NY, NX, 16, small), BF16),
            pltpu.VMEM((steps, 16, 2 * width), BF16),
            pltpu.VMEM((steps, 16, small), BF16),
            pltpu.VMEM((steps, 16, 2 * width), BF16),
            pltpu.VMEM((steps, 16, small), BF16),
            pltpu.VMEM((NX, 2, 16, width), F32),
            pltpu.VMEM((NX, 16, small), F32),
            pltpu.VMEM((3, 16, width), BF16),
            pltpu.VMEM((3, 16, width), BF16),
            pltpu.VMEM((3, 16, 128), BF16),
            pltpu.VMEM((3, 16, 128), BF16),
            pltpu.VMEM((16, half), BF16),
            pltpu.VMEM((16, half), BF16),
            pltpu.VMEM((tiles + 1, 16, 128), BF16),
            pltpu.VMEM((n_dp // 2, 16, 128), BF16),
            pltpu.VMEM((2 * tiles + 1, 16, 128), BF16),
            dma((12,)),
            dma((NY,)),
            dma((NY,)),
            dma((NY,)),
            dma((NY,)),
            dma((2 * NY,)),
            dma((2 * NY,)),
            dma((2, NY)),
            dma((2, NY)),
            dma((2, steps)),
            dma((2, steps)),
            dma((2, steps)),
            dma((2, steps)),
            dma((3, 3)),
            dma((3, 3)),
            dma((tiles + 1,)),
            dma((n_dp // 2,)),
            dma((n_dp,)),
            dma((2 * tiles + 1,)),
        ],
        compiler_params=pltpu.CompilerParams(
            collective_id=0, has_side_effects=True, vmem_limit_bytes=60 * 1024 * 1024
        ),
    )(
        atom_h[0],
        edge_x[0],
        edge_source,
        edge_target,
        trip_in,
        trip_out,
        basis[0],
        block_counts,
        atom_cotangent[0],
        weight_edge,
        weight_basis,
    )
    grad_x, grad_h, grad_w, grad_wb = pl.pallas_call(
        write_out,
        out_shape=(
            jax.ShapeDtypeStruct((edges, width), BF16),
            jax.ShapeDtypeStruct((atoms_dev, width), BF16),
            jax.ShapeDtypeStruct((owned, width), F32),
            jax.ShapeDtypeStruct((owned, nb), F32),
        ),
        in_specs=[hbm] * 4,
        out_specs=(hbm, hbm, hbm, hbm),
        scratch_shapes=[
            pltpu.VMEM((edges, width), BF16),
            pltpu.VMEM((atoms_dev, width), BF16),
            pltpu.VMEM((owned, width), F32),
            pltpu.VMEM((16, 128), F32),
            pltpu.VMEM((owned, nb), F32),
            dma((7,)),
            dma((7,)),
        ],
        compiler_params=pltpu.CompilerParams(
            has_side_effects=True, vmem_limit_bytes=60 * 1024 * 1024
        ),
    )(grad_x, grad_h, grad_w, grad_wb)
    return (grad_x[None], grad_h[None], grad_w, grad_wb.T)


def solution(mesh):
    placed = (
        P("dp", "graph", None),
        P("dp", "graph", None),
        P("dp", "graph"),
        P("dp", "graph"),
        P("dp", "graph"),
        P("dp", "graph"),
        P("dp", None, "graph"),
        P("dp", "graph"),
        P("dp", "graph", None),
        P(),
        P(),
    )
    return jax.shard_map(
        shards,
        mesh=mesh,
        in_specs=placed,
        out_specs=(
            P("dp", "graph", None),
            P("dp", "graph", None),
            P("graph", None),
            P(None, "graph"),
        ),
        check_vma=False,
    )
```

time: 89.5 us -> 85.4 us (0.954)
  local copies, waits for them, and re-layouts: 11.1 us -> 0 us
  Pallas kernels: 76.1 us -> 83.8 us
    unnamed x23 -> x0, local copies, waits for them, and re-layouts: 11 us -> none
    pallas_call x1, Pallas kernels: 76.1 us -> 81.7 us  [shards(): pl.pallas_call(lambda *refs: kernel(n_dp, *refs), out_shape=(jax.ShapeDty...]
    pallas_call x0 -> x1, Pallas kernels: none -> 2.13 us  [shards(): pl.pallas_call(write_out, out_shape=(jax.ShapeDtypeStruct((edges, width),...]
where the time goes in v2:
time: 85.4 us; the launch traced here: 85.1 us
  Pallas kernels  83.8 us (98%)
  between operations  1.29 us (2%)
    pallas_call x1, Pallas kernels, shards(): pl.pallas_call(lambda *refs: kernel(n_dp, *refs), out_shape=(jax.ShapeDty...  81.7 us
    pallas_call x1, Pallas kernels, shards(): pl.pallas_call(write_out, out_shape=(jax.ShapeDtypeStruct((edges, width),...  2.13 us

profile of v2, /device:TPU:2, one launch (start us, length us, event | category | flops | bytes accessed | tf_op | source)
XLA Modules:
  0.0 85.1 jit_solution(5070713621708301011)
XLA Ops:
  1.3 81.7 %shard_map.138 = (bf16[512,1024]{1,0:T(8,128)(2,1)}, bf16[8,1024]{1,0:T(8,128)(2,1)}, f32[32,1024]{1,0:T(8,128)}, f32[16,128]{1,0:T(8,128)}) custom-call(bf16[8,1024]{1,0:T(8,128)(2,1)} %bitcast.9, bf16[512,1024]{1,0:T(8,128)(2,1)} %bitcast.7, s32[1,512]{1,0:T(1,128)} %refs_2_.1, s32[1,512]{1,0:T(1,128)} %refs_3_.1, s32[1,1024]{1,0:T(1,128)} %refs_4_.1, ...), custom_call_target="tpu_custom_call" | custom-call | tf_op jit(solution)/shard_map/pallas_call | solution.py:610
  83.0 2.1 %shard_map.139 = (bf16[512,1024]{1,0:T(8,128)(2,1)}, bf16[8,1024]{1,0:T(8,128)(2,1)}, f32[32,1024]{1,0:T(8,128)}, f32[32,64]{1,0:T(8,128)}) custom-call(bf16[512,1024]{1,0:T(8,128)(2,1)} %get-tuple-element.12.gx, bf16[8,1024]{1,0:T(8,128)(2,1)} %get-tuple-element.13.gh, f32[32,1024]{1,0:T(8,128)} %get-tuple-element.14.gw, f32[16,128]{1,0:T(8,128)} %get-tuple-element.15.gwb), custom_call_target="tpu_custom_call" | custom-call | tf_op jit(solution)/shard_map/pallas_call | solution.py:696

commit v3 on v2

--- a/solution.py
+++ b/solution.py
@@ -182,48 +182,6 @@
     hrows = h_ref[...].astype(F32)
     own_rows = jnp.concatenate([hrows[:, :half], hrows[:, half:]], axis=0).astype(BF16)
     table[xl, y, c] = own_rows
-    pl.semaphore_wait(barrier, len(greeted) + n_dp - 1)
-
-    def block(offset, part=None):
-        if part is None:
-            return table.at[xl, along(offset), c]
-        return table.at[xl, along(offset), c, :, part * (half // 2) : (part + 1) * (half // 2)]
-
-    number = {-1: 0, -2: 1, 1: 2, 2: 3, -3: 4, 3: 5, -4: 6, 4: 7}
-    side = {-4: 0, 4: 1}
-
-    def table_send(offset, to):
-        seen = offset - to
-        i, ref = number[seen], block(offset, side.get(seen))
-        begin(remote(ref, ref, tab_send.at[i], tab_recv.at[i], y_peer(to)))
-
-    def table_wait(seen):
-        i, ref = number[seen], block(seen, side.get(seen))
-        remote(ref, ref, tab_send.at[i], tab_recv.at[i], sibling).wait_recv()
-
-    def across_send(i):
-        ref = block(PLACES[i])
-        begin(remote(ref, ref, tabx_send.at[i], tabx_recv.at[i], across))
-
-    def across_wait(i):
-        ref = table.at[1 - xl, along(PLACES[i]), c]
-        remote(ref, ref, tabx_send.at[i], tabx_recv.at[i], sibling).wait_recv()
-
-    def sibling_send(i, other):
-        ref = table.at[(1 - xl) if other else xl, along(PLACES[i]), c]
-        j = other * NY + i
-        begin(remote(ref, ref, sib_send.at[j], sib_recv.at[j], sibling))
-
-    def sibling_wait(i, other):
-        ref = table.at[(1 - xl) if other else xl, along(PLACES[i]), oc]
-        j = other * NY + i
-        remote(ref, ref, sib_send.at[j], sib_recv.at[j], sibling).wait_recv()
-
-    for to in (2, -2, 1, -1):
-        table_send(0, to)
-    across_send(0)
-    sibling_send(0, 0)
-
     for load in loads[1:-2]:
         load.wait()
     edge_of_slot = lax.broadcasted_iota(jnp.int32, (edges, trips), 0)
@@ -238,6 +196,48 @@
     a_of = dot(target_hits, hits_out)
     slot = lax.broadcasted_iota(jnp.int32, (1, trips), 1)
     a_of = jnp.where(slot < counts_ref[0, 0] * BLOCK, a_of, 0.0)
+
+    pl.semaphore_wait(barrier, len(greeted) + n_dp - 1)
+
+    def block(offset, part=None):
+        if part is None:
+            return table.at[xl, along(offset), c]
+        return table.at[xl, along(offset), c, :, part * (half // 2) : (part + 1) * (half // 2)]
+
+    number = {-1: 0, -2: 1, 1: 2, 2: 3, -3: 4, 3: 5, -4: 6, 4: 7}
+    side = {-4: 0, 4: 1}
+
+    def table_send(offset, to):
+        seen = offset - to
+        i, ref = number[seen], block(offset, side.get(seen))
+        begin(remote(ref, ref, tab_send.at[i], tab_recv.at[i], y_peer(to)))
+
+    def table_wait(seen):
+        i, ref = number[seen], block(seen, side.get(seen))
+        remote(ref, ref, tab_send.at[i], tab_recv.at[i], sibling).wait_recv()
+
+    def across_send(i):
+        ref = block(PLACES[i])
+        begin(remote(ref, ref, tabx_send.at[i], tabx_recv.at[i], across))
+
+    def across_wait(i):
+        ref = table.at[1 - xl, along(PLACES[i]), c]
+        remote(ref, ref, tabx_send.at[i], tabx_recv.at[i], sibling).wait_recv()
+
+    def sibling_send(i, other):
+        ref = table.at[(1 - xl) if other else xl, along(PLACES[i]), c]
+        j = other * NY + i
+        begin(remote(ref, ref, sib_send.at[j], sib_recv.at[j], sibling))
+
+    def sibling_wait(i, other):
+        ref = table.at[(1 - xl) if other else xl, along(PLACES[i]), oc]
+        j = other * NY + i
+        remote(ref, ref, sib_send.at[j], sib_recv.at[j], sibling).wait_recv()
+
+    for to in (2, -2, 1, -1):
+        table_send(0, to)
+    across_send(0)
+    sibling_send(0, 0)
 
     for seen, to in ((-2, 1), (2, -1), (-2, 2), (2, -2)):
         if abs(to) == 1:
@@ -421,28 +421,33 @@
                 BF16
             )
 
+    grad_x_piece(0)
+    grad_x_piece(1)
+    grad_x_piece(2)
+    grad_x_piece(3)
+    store_gx = pltpu.make_async_copy(gx_ref, gx_hbm, load_sem.at[11])
+    store_gx.start()
+    atoms_piece()
+    basis_piece(0)
+    basis_piece(1)
+    basis_piece(2)
+    basis_piece(3)
+    for m in (4, 3, 5, 2, 6, 1, 7, 0):
+        begin(core_copy(part_s, core_s, 1, along(m - NY)))
     step_w(0)
     step_w(1)
-    grad_x_piece(0)
-    grad_x_piece(1)
-    step_w(2)
-    grad_x_piece(2)
-    grad_x_piece(3)
-    step_w(3)
-    store_gx = pltpu.make_async_copy(gx_ref, gx_hbm, load_sem.at[11])
-    store_gx.start()
-    basis_piece(0)
-    basis_piece(1)
-    step_w(4)
-    basis_piece(2)
-    basis_piece(3)
-    step_w(5)
-    atoms_piece()
-    for m in (4, 3, 5, 2, 6, 1, 7, 0):
-        begin(core_copy(part_s, core_s, 1, along(m - NY)))
-    step_w(6)
     step_s(0)
     step_s(1)
+    step_w(2)
+    step_s(2)
+    step_w(3)
+    step_s(3)
+    step_w(4)
+    step_s(4)
+    step_w(5)
+    step_s(5)
+    step_w(6)
+    step_s(6)
 
     for px, value in enumerate(finish_w()):
         acc_w[px, 0] = value[:, :width]
@@ -462,8 +467,6 @@
     for p, (qx, qh) in enumerate(quarters):
         x_out_w[p] = acc_w[qx, qh].astype(BF16)
         begin(x_copy_w(p))
-    for k in range(2, len(DIST)):
-        step_s(k)
     for px, value in enumerate(finish_s()):
         acc_s[px] = value
     for p, (qx, qh) in enumerate(quarters):

time: 85.4 us -> 77.4 us (0.906)
  Pallas kernels: 83.8 us -> 75.9 us
    pallas_call x1, Pallas kernels: 81.7 us -> 73.8 us  [shards(): pl.pallas_call(lambda *refs: kernel(n_dp, *refs), out_shape=(jax.ShapeDty...]
where the time goes in v3:
time: 77.4 us; the launch traced here: 77.2 us
  Pallas kernels  75.9 us (98%)
  between operations  1.29 us (2%)
    pallas_call x1, Pallas kernels, shards(): pl.pallas_call(lambda *refs: kernel(n_dp, *refs), out_shape=(jax.ShapeDty...  73.8 us
    pallas_call x1, Pallas kernels, shards(): pl.pallas_call(write_out, out_shape=(jax.ShapeDtypeStruct((edges, width),...  2.13 us

profile of v3, /device:TPU:2, one launch (start us, length us, event | category | flops | bytes accessed | tf_op | source)
XLA Modules:
  0.0 77.2 jit_solution(18442123301852662416)
XLA Ops:
  1.3 73.8 %shard_map.138 = (bf16[512,1024]{1,0:T(8,128)(2,1)}, bf16[8,1024]{1,0:T(8,128)(2,1)}, f32[32,1024]{1,0:T(8,128)}, f32[16,128]{1,0:T(8,128)}) custom-call(bf16[8,1024]{1,0:T(8,128)(2,1)} %bitcast.9, bf16[512,1024]{1,0:T(8,128)(2,1)} %bitcast.7, s32[1,512]{1,0:T(1,128)} %refs_2_.1, s32[1,512]{1,0:T(1,128)} %refs_3_.1, s32[1,1024]{1,0:T(1,128)} %refs_4_.1, ...), custom_call_target="tpu_custom_call" | custom-call | tf_op jit(solution)/shard_map/pallas_call | solution.py:613
  75.1 2.1 %shard_map.139 = (bf16[512,1024]{1,0:T(8,128)(2,1)}, bf16[8,1024]{1,0:T(8,128)(2,1)}, f32[32,1024]{1,0:T(8,128)}, f32[32,64]{1,0:T(8,128)}) custom-call(bf16[512,1024]{1,0:T(8,128)(2,1)} %get-tuple-element.12.gx, bf16[8,1024]{1,0:T(8,128)(2,1)} %get-tuple-element.13.gh, f32[32,1024]{1,0:T(8,128)} %get-tuple-element.14.gw, f32[16,128]{1,0:T(8,128)} %get-tuple-element.15.gwb), custom_call_target="tpu_custom_call" | custom-call | tf_op jit(solution)/shard_map/pallas_call | solution.py:699

commit v4 on v3

--- a/solution.py
+++ b/solution.py
@@ -141,6 +141,13 @@
             device_id_type=MESH,
         )
 
+    steps_z = sorted(range(nz), key=lambda k: -min(k, nz - k))
+    far_first = [(k, flip) for k in steps_z for flip in (1, 0) if k or flip]
+
+    def z_peer(step, flip=0):
+        side = (1 - xh) if flip else xh
+        return {"dp": side * nz + lax.rem(z + step, nz)}
+
     sent = []
 
     def begin(copy):
@@ -170,13 +177,12 @@
     load_h, load_x, load_we = loads[0], loads[-2], loads[-1]
 
     barrier = pltpu.get_barrier_semaphore()
-    greeted = [sibling, right, left, y_peer(2), y_peer(-2), across, x_peers[2]]
+    greeted = [y_peer(k) for k in (4, 3, -3, 2, -2, 1, -1)] + [sibling, across, x_peers[2]]
     for peer in greeted:
         signal(barrier, peer)
 
-    @pl.loop(1, n_dp)
-    def _(k):
-        signal(barrier, {"dp": lax.rem(dp + k, n_dp)})
+    for step, flip in far_first:
+        signal(barrier, z_peer(step, flip))
 
     load_h.wait()
     hrows = h_ref[...].astype(F32)
@@ -199,21 +205,15 @@
 
     pl.semaphore_wait(barrier, len(greeted) + n_dp - 1)
 
-    def block(offset, part=None):
-        if part is None:
-            return table.at[xl, along(offset), c]
-        return table.at[xl, along(offset), c, :, part * (half // 2) : (part + 1) * (half // 2)]
-
-    number = {-1: 0, -2: 1, 1: 2, 2: 3, -3: 4, 3: 5, -4: 6, 4: 7}
-    side = {-4: 0, 4: 1}
-
-    def table_send(offset, to):
-        seen = offset - to
-        i, ref = number[seen], block(offset, side.get(seen))
+    def block(offset):
+        return table.at[xl, along(offset), c]
+
+    def table_send(to):
+        i, ref = PLACES.index(4 if to == 4 else -to), block(0)
         begin(remote(ref, ref, tab_send.at[i], tab_recv.at[i], y_peer(to)))
 
-    def table_wait(seen):
-        i, ref = number[seen], block(seen, side.get(seen))
+    def table_wait(i):
+        ref = block(PLACES[i])
         remote(ref, ref, tab_send.at[i], tab_recv.at[i], sibling).wait_recv()
 
     def across_send(i):
@@ -234,21 +234,10 @@
         j = other * NY + i
         remote(ref, ref, sib_send.at[j], sib_recv.at[j], sibling).wait_recv()
 
-    for to in (2, -2, 1, -1):
-        table_send(0, to)
+    for to in (4, 3, -3, 2, -2, 1, -1):
+        table_send(to)
     across_send(0)
     sibling_send(0, 0)
-
-    for seen, to in ((-2, 1), (2, -1), (-2, 2), (2, -2)):
-        if abs(to) == 1:
-            table_wait(seen)
-        table_send(seen, to)
-    table_wait(-1)
-    table_wait(1)
-    for i in (2, 4, 1, 3):
-        across_send(i)
-    for i in (2, 4, 1, 3):
-        sibling_send(i, 0)
 
     hits_in = (edge_of_slot == tin_ref[...] - edge_base).astype(F32).astype(BF16)
     basis = basis_ref[...].astype(F32)
@@ -259,15 +248,10 @@
         ).astype(BF16)
         mt_ref[:, q * 256 : (q + 1) * 256] = dot(hits_in, spreadout, NT).astype(BF16)
 
-    for seen in (-3, 3, -4, 4):
-        table_wait(seen)
-    for i in (5, 6, 7):
+    for i in (1, 3, 2, 4, 5, 6, 7):
+        table_wait(i)
         across_send(i)
-    for i in (5, 6, 7):
         sibling_send(i, 0)
-    for i in (0, 2, 4, 1, 3):
-        across_wait(i)
-        sibling_send(i, 1)
 
     cot = cot_ref[...].astype(F32)
     wb = wb_ref[...].astype(F32)
@@ -277,7 +261,7 @@
         js = slice(j * 256, (j + 1) * 256)
         gm_ref[:, js] = dot(mt_ref[...], g_ref[:, js])
 
-    for i in (5, 6, 7):
+    for i in (0, 1, 3, 2, 4, 5, 6, 7):
         across_wait(i)
         sibling_send(i, 1)
     for i in range(NY):
@@ -421,6 +405,8 @@
                 BF16
             )
 
+    step_w(0)
+    step_w(1)
     grad_x_piece(0)
     grad_x_piece(1)
     grad_x_piece(2)
@@ -434,24 +420,19 @@
     basis_piece(3)
     for m in (4, 3, 5, 2, 6, 1, 7, 0):
         begin(core_copy(part_s, core_s, 1, along(m - NY)))
-    step_w(0)
-    step_w(1)
     step_s(0)
     step_s(1)
     step_w(2)
     step_s(2)
     step_w(3)
     step_s(3)
+    step_s(4)
     step_w(4)
-    step_s(4)
+    step_s(5)
     step_w(5)
-    step_s(5)
+    step_s(6)
     step_w(6)
-    step_s(6)
-
-    for px, value in enumerate(finish_w()):
-        acc_w[px, 0] = value[:, :width]
-        acc_w[px, 1] = value[:, width:]
+
     quarters = ((1 - xl, xh), (xl, 1 - xh), (1 - xl, 1 - xh))
 
     def x_copy(kind, p, out, landing):
@@ -464,14 +445,17 @@
         return x_copy(1, p, x_out_b.at[p], x_in_b.at[p])
 
     x_copy_h = x_copy(2, 0, x_out_h, x_in_h)
-    for p, (qx, qh) in enumerate(quarters):
-        x_out_w[p] = acc_w[qx, qh].astype(BF16)
-        begin(x_copy_w(p))
     for px, value in enumerate(finish_s()):
         acc_s[px] = value
     for p, (qx, qh) in enumerate(quarters):
         x_out_b[p] = acc_s[qx, :, :128].astype(BF16)
         begin(x_copy_b(p))
+    for px, value in enumerate(finish_w()):
+        acc_w[px, 0] = value[:, :width]
+        acc_w[px, 1] = value[:, width:]
+    for p, (qx, qh) in enumerate(quarters):
+        x_out_w[p] = acc_w[qx, qh].astype(BF16)
+        begin(x_copy_w(p))
     x_out_h[...] = acc_s[1 - xl, :, 128:].astype(BF16)
     begin(x_copy_h)
 
@@ -489,16 +473,18 @@
     dp_out[tiles] = total_b.astype(BF16)
     mine = tiles + xh
 
-    def share(t):
-        return remote(
-            dp_out.at[t], dp_in.at[z], dps_send.at[t], dps_recv.at[z], {"dp": xh * nz + t}
+    def share(step):
+        t = lax.rem(z + step, nz)
+        return t, remote(
+            dp_out.at[t], dp_in.at[z], dps_send.at[t], dps_recv.at[z], z_peer(step)
         )
 
-    @pl.loop(0, mine)
-    def _(t):
-        @pl.when(t != z)
-        def _():
-            share(t).start()
+    for step in steps_z[:-1]:
+        tile, copy = share(step)
+
+        @pl.when(tile < mine)
+        def _(copy=copy):
+            copy.start()
 
     x_copy_h.wait_recv()
     grad_h = acc_s[xl, :, 128:] + x_in_h[...].astype(F32)
@@ -508,14 +494,16 @@
 
     own_tile = xh * tiles + z
 
-    def spread_total(k):
-        return remote(
+    totals = [
+        remote(
             dp_all.at[own_tile],
             dp_all.at[own_tile],
             dpg_send.at[k],
             dpg_recv.at[own_tile],
-            {"dp": lax.rem(dp + k, n_dp)},
+            z_peer(step, flip),
         )
+        for k, (step, flip) in enumerate(far_first)
+    ]
 
     @pl.when(z < mine)
     def _():
@@ -530,9 +518,8 @@
 
         dp_all[own_tile] = jnp.sum(dp_in[...].astype(F32), axis=0).astype(BF16)
 
-        @pl.loop(1, n_dp)
-        def _(k):
-            spread_total(k).start()
+        for copy in totals:
+            copy.start()
 
     @pl.loop(0, 2 * tiles + 1)
     def _(t):
@@ -549,15 +536,15 @@
 
     @pl.when(z < mine)
     def _():
-        @pl.loop(1, n_dp)
-        def _(k):
-            spread_total(k).wait_send()
-
-    @pl.loop(0, mine)
-    def _(t):
-        @pl.when(t != z)
-        def _():
-            share(t).wait_send()
+        for copy in totals:
+            copy.wait_send()
+
+    for step in steps_z[:-1]:
+        tile, copy = share(step)
+
+        @pl.when(tile < mine)
+        def _(copy=copy):
+            copy.wait_send()
 
     for copy in sent:
         copy.wait_send()
@@ -657,9 +644,9 @@
             pltpu.VMEM((3, 16, 128), BF16),
             pltpu.VMEM((16, half), BF16),
             pltpu.VMEM((16, half), BF16),
-            pltpu.VMEM((tiles + 1, 16, 128), BF16),
             pltpu.VMEM((n_dp // 2, 16, 128), BF16),
-            pltpu.VMEM((2 * tiles + 1, 16, 128), BF16),
+            pltpu.VMEM((n_dp // 2, 16, 128), BF16),
+            pltpu.VMEM((n_dp, 16, 128), BF16),
             dma((12,)),
             dma((NY,)),
             dma((NY,)),
@@ -675,10 +662,10 @@
             dma((2, steps)),
             dma((3, 3)),
             dma((3, 3)),
-            dma((tiles + 1,)),
+            dma((n_dp // 2,)),
             dma((n_dp // 2,)),
             dma((n_dp,)),
-            dma((2 * tiles + 1,)),
+            dma((n_dp,)),
         ],
         compiler_params=pltpu.CompilerParams(
             collective_id=0, has_side_effects=True, vmem_limit_bytes=60 * 1024 * 1024

time: 77.4 us -> 74.4 us (0.961)
  Pallas kernels: 75.9 us -> 72.9 us
    pallas_call x1, Pallas kernels: 73.8 us -> 70.7 us  [shards(): pl.pallas_call(lambda *refs: kernel(n_dp, *refs), out_shape=(jax.ShapeDty...]
where the time goes in v4:
time: 74.4 us; the launch traced here: 74.1 us
  Pallas kernels  72.9 us (98%)
  between operations  1.29 us (2%)
    pallas_call x1, Pallas kernels, shards(): pl.pallas_call(lambda *refs: kernel(n_dp, *refs), out_shape=(jax.ShapeDty...  70.7 us
    pallas_call x1, Pallas kernels, shards(): pl.pallas_call(write_out, out_shape=(jax.ShapeDtypeStruct((edges, width),...  2.13 us

profile of v4, /device:TPU:2, one launch (start us, length us, event | category | flops | bytes accessed | tf_op | source)
XLA Modules:
  0.0 74.1 jit_solution(10985523628942398908)
XLA Ops:
  1.3 70.7 %shard_map.138 = (bf16[512,1024]{1,0:T(8,128)(2,1)}, bf16[8,1024]{1,0:T(8,128)(2,1)}, f32[32,1024]{1,0:T(8,128)}, f32[16,128]{1,0:T(8,128)}) custom-call(bf16[8,1024]{1,0:T(8,128)(2,1)} %bitcast.9, bf16[512,1024]{1,0:T(8,128)(2,1)} %bitcast.7, s32[1,512]{1,0:T(1,128)} %refs_2_.1, s32[1,512]{1,0:T(1,128)} %refs_3_.1, s32[1,1024]{1,0:T(1,128)} %refs_4_.1, ...), custom_call_target="tpu_custom_call" | custom-call | tf_op jit(solution)/shard_map/pallas_call | solution.py:600
  72.0 2.1 %shard_map.139 = (bf16[512,1024]{1,0:T(8,128)(2,1)}, bf16[8,1024]{1,0:T(8,128)(2,1)}, f32[32,1024]{1,0:T(8,128)}, f32[32,64]{1,0:T(8,128)}) custom-call(bf16[512,1024]{1,0:T(8,128)(2,1)} %get-tuple-element.12.gx, bf16[8,1024]{1,0:T(8,128)(2,1)} %get-tuple-element.13.gh, f32[32,1024]{1,0:T(8,128)} %get-tuple-element.14.gw, f32[16,128]{1,0:T(8,128)} %get-tuple-element.15.gwb), custom_call_target="tpu_custom_call" | custom-call | tf_op jit(solution)/shard_map/pallas_call | solution.py:686

commit v5 on v4

--- a/solution.py
+++ b/solution.py
@@ -54,6 +54,7 @@
     table,
     tab,
     mt_ref,
+    m_ref,
     g_ref,
     gm_ref,
     joined_ref,
@@ -61,15 +62,20 @@
     gx_ref,
     msg_ref,
     part_w,
-    part_s,
+    part_b,
+    part_h,
     core_w,
-    core_s,
+    core_b,
+    core_h,
     left_w,
-    left_s,
+    left_b,
+    left_h,
     right_w,
-    right_s,
+    right_b,
+    right_h,
     acc_w,
-    acc_s,
+    acc_b,
+    acc_h,
     x_out_w,
     x_in_w,
     x_out_b,
@@ -154,6 +160,14 @@
         copy.start()
         sent.append(copy)
 
+    barrier = pltpu.get_barrier_semaphore()
+    greeted = [y_peer(k) for k in (4, 3, -3, 2, -2, 1, -1)] + [sibling, across, x_peers[2]]
+    for peer in greeted:
+        signal(barrier, peer)
+
+    for step, flip in far_first:
+        signal(barrier, z_peer(step, flip))
+
     loads = [
         pltpu.make_async_copy(src, dst, load_sem.at[i])
         for i, (src, dst) in enumerate(
@@ -176,14 +190,6 @@
         load.start()
     load_h, load_x, load_we = loads[0], loads[-2], loads[-1]
 
-    barrier = pltpu.get_barrier_semaphore()
-    greeted = [y_peer(k) for k in (4, 3, -3, 2, -2, 1, -1)] + [sibling, across, x_peers[2]]
-    for peer in greeted:
-        signal(barrier, peer)
-
-    for step, flip in far_first:
-        signal(barrier, z_peer(step, flip))
-
     load_h.wait()
     hrows = h_ref[...].astype(F32)
     own_rows = jnp.concatenate([hrows[:, :half], hrows[:, half:]], axis=0).astype(BF16)
@@ -247,6 +253,7 @@
             [basis * a_of[a : a + 1, :] for a in range(q * group, (q + 1) * group)], axis=0
         ).astype(BF16)
         mt_ref[:, q * 256 : (q + 1) * 256] = dot(hits_in, spreadout, NT).astype(BF16)
+        m_ref[q * 256 : (q + 1) * 256, :] = dot(spreadout, hits_in, NT).astype(BF16)
 
     for i in (1, 3, 2, 4, 5, 6, 7):
         table_wait(i)
@@ -261,6 +268,14 @@
         js = slice(j * 256, (j + 1) * 256)
         gm_ref[:, js] = dot(mt_ref[...], g_ref[:, js])
 
+    all_atoms = NX * NY * NC * atoms_dev
+    atom_of_edge = lax.broadcasted_iota(jnp.int32, (all_atoms, edges), 0)
+    ends_of = (atom_of_edge == src_ref[...]).astype(F32) + (
+        atom_of_edge == tgt_ref[...]
+    ).astype(F32)
+    hits = ends_of.astype(BF16)
+    hits_t = ends_of.T.astype(BF16)
+
     for i in (0, 1, 3, 2, 4, 5, 6, 7):
         across_wait(i)
         sibling_send(i, 1)
@@ -268,25 +283,20 @@
         sibling_wait(i, 0)
         sibling_wait(i, 1)
 
-    all_atoms = NX * NY * NC * atoms_dev
     packed = table[...].astype(F32).reshape(NX * NY * NC, 2 * atoms_dev, half)
     tab[:, :half] = packed[:, :atoms_dev, :].reshape(all_atoms, half).astype(BF16)
     tab[:, half:] = packed[:, atoms_dev:, :].reshape(all_atoms, half).astype(BF16)
 
-    atom_of_edge = lax.broadcasted_iota(jnp.int32, (all_atoms, edges), 0)
-    hits = (
-        (atom_of_edge == src_ref[...]).astype(F32) + (atom_of_edge == tgt_ref[...]).astype(F32)
-    ).astype(BF16)
     load_x.wait()
     for j in range(width // 256):
         js = slice(j * 256, (j + 1) * 256)
-        ends = dot(hits, tab[:, js], TN)
+        ends = dot(hits_t, tab[:, js])
         joined_ref[:, js] = (x_ref[:, js].astype(F32) + ends).astype(BF16)
     load_we.wait()
     for j in range(width // 256):
         js = slice(j * 256, (j + 1) * 256)
         pre = dot(joined_ref[...], we_ref[:, js])
-        logistic = 1.0 / (1.0 + jnp.exp(-pre))
+        logistic = 0.5 + 0.5 * jnp.tanh(0.5 * pre)
         msg_ref[:, js] = (pre * logistic).astype(BF16)
         slope = logistic * (1.0 + pre * (1.0 - logistic))
         gp_ref[:, js] = (gm_ref[:, js] * slope).astype(BF16)
@@ -374,14 +384,15 @@
         return step, finish
 
     step_w, finish_w = stream(0, part_w, core_w, left_w, right_w)
-    step_s, finish_s = stream(1, part_s, core_s, left_s, right_s)
+    step_b, finish_b = stream(1, part_b, core_b, left_b, right_b)
+    step_h, finish_h = stream(2, part_h, core_h, left_h, right_h)
 
     def owner_of(number):
         return (number // NC) % NY, number // (NC * NY), number % NC
 
     def basis_piece(j):
         js = slice(j * 256, (j + 1) * 256)
-        spread_sum = dot(mt_ref[...], msg_ref[:, js], TN)
+        spread_sum = dot(m_ref[...], msg_ref[:, js])
         gwb = jnp.zeros((nb, 256), F32)
         for a in range(atoms_dev):
             gwb = gwb + spread_sum[a * nb : (a + 1) * nb, :] * cot[a : a + 1, js]
@@ -389,7 +400,7 @@
         turned = both.T.astype(BF16).reshape(8, 2, 16, 128)
         for k in range(8):
             py, px, pc = owner_of(j * 8 + k)
-            part_s[py, px, pc, :, :128] = turned[k, 0]
+            part_b[py, px, pc] = turned[k, 0]
 
     def grad_x_piece(j):
         js = slice(j * 256, (j + 1) * 256)
@@ -401,10 +412,17 @@
         for number in range(NX * NY * NC):
             py, px, pc = owner_of(number)
             rows = slice(number * atoms_dev, (number + 1) * atoms_dev)
-            part_s[py, px, pc, :, 128:] = jnp.concatenate([lo[rows], hi[rows]], axis=0).astype(
-                BF16
-            )
-
+            part_h[py, px, pc] = jnp.concatenate([lo[rows], hi[rows]], axis=0).astype(BF16)
+
+    def share_cores(sem, part, landing):
+        for m in (4, 3, 5, 2, 6, 1, 7, 0):
+            begin(core_copy(part, landing, sem, along(m - NY)))
+
+    basis_piece(0)
+    basis_piece(1)
+    basis_piece(2)
+    basis_piece(3)
+    share_cores(1, part_b, core_b)
     step_w(0)
     step_w(1)
     grad_x_piece(0)
@@ -414,23 +432,22 @@
     store_gx = pltpu.make_async_copy(gx_ref, gx_hbm, load_sem.at[11])
     store_gx.start()
     atoms_piece()
-    basis_piece(0)
-    basis_piece(1)
-    basis_piece(2)
-    basis_piece(3)
-    for m in (4, 3, 5, 2, 6, 1, 7, 0):
-        begin(core_copy(part_s, core_s, 1, along(m - NY)))
-    step_s(0)
-    step_s(1)
+    share_cores(2, part_h, core_h)
+    step_b(0)
+    step_b(1)
     step_w(2)
-    step_s(2)
+    step_b(2)
+    step_h(0)
     step_w(3)
-    step_s(3)
-    step_s(4)
+    step_b(3)
+    step_h(1)
+    step_b(4)
     step_w(4)
-    step_s(5)
+    step_b(5)
+    step_h(2)
     step_w(5)
-    step_s(6)
+    step_b(6)
+    step_h(3)
     step_w(6)
 
     quarters = ((1 - xl, xh), (xl, 1 - xh), (1 - xl, 1 - xh))
@@ -445,10 +462,10 @@
         return x_copy(1, p, x_out_b.at[p], x_in_b.at[p])
 
     x_copy_h = x_copy(2, 0, x_out_h, x_in_h)
-    for px, value in enumerate(finish_s()):
-        acc_s[px] = value
+    for px, value in enumerate(finish_b()):
+        acc_b[px] = value
     for p, (qx, qh) in enumerate(quarters):
-        x_out_b[p] = acc_s[qx, :, :128].astype(BF16)
+        x_out_b[p] = acc_b[qx].astype(BF16)
         begin(x_copy_b(p))
     for px, value in enumerate(finish_w()):
         acc_w[px, 0] = value[:, :width]
@@ -456,11 +473,9 @@
     for p, (qx, qh) in enumerate(quarters):
         x_out_w[p] = acc_w[qx, qh].astype(BF16)
         begin(x_copy_w(p))
-    x_out_h[...] = acc_s[1 - xl, :, 128:].astype(BF16)
-    begin(x_copy_h)
 
     total_w = acc_w[xl, xh]
-    total_b = acc_s[xl, :, :128]
+    total_b = acc_b[xl]
     for p in range(3):
         x_copy_w(p).wait_recv()
         total_w = total_w + x_in_w[p].astype(F32)
@@ -486,11 +501,9 @@
         def _(copy=copy):
             copy.start()
 
-    x_copy_h.wait_recv()
-    grad_h = acc_s[xl, :, 128:] + x_in_h[...].astype(F32)
-    gh_ref[...] = (
-        cot + jnp.concatenate([grad_h[:atoms_dev], grad_h[atoms_dev:]], axis=1)
-    ).astype(BF16)
+    step_h(4)
+    step_h(5)
+    step_h(6)
 
     own_tile = xh * tiles + z
 
@@ -521,6 +534,11 @@
         for copy in totals:
             copy.start()
 
+    for px, value in enumerate(finish_h()):
+        acc_h[px] = value
+    x_out_h[...] = acc_h[1 - xl].astype(BF16)
+    begin(x_copy_h)
+
     @pl.loop(0, 2 * tiles + 1)
     def _(t):
         @pl.when(jnp.logical_or(t != own_tile, z >= mine))
@@ -533,6 +551,12 @@
         r, q = t // tiles, t % tiles
         gw_ref[r * 16 : (r + 1) * 16, q * 128 : (q + 1) * 128] = dp_all[t].astype(F32)
     gwb_ref[...] = dp_all[2 * tiles].astype(F32)
+
+    x_copy_h.wait_recv()
+    grad_h = acc_h[xl] + x_in_h[...].astype(F32)
+    gh_ref[...] = (
+        cot + jnp.concatenate([grad_h[:atoms_dev], grad_h[atoms_dev:]], axis=1)
+    ).astype(BF16)
 
     @pl.when(z < mine)
     def _():
@@ -591,7 +615,6 @@
     atoms_dev = atom_h.shape[1]
     owned = width // (NX * NY * NC)
     half = width // 2
-    small = 128 + half
     steps = len(DIST)
     tiles = width // 128
     vmem = pl.BlockSpec(memory_space=pltpu.VMEM)
@@ -622,6 +645,7 @@
             pltpu.VMEM((NX, NY, NC, 2 * atoms_dev, half), BF16),
             pltpu.VMEM((NX * NY * NC * atoms_dev, width), BF16),
             pltpu.VMEM((edges, atoms_dev * nb), BF16),
+            pltpu.VMEM((atoms_dev * nb, edges), BF16),
             pltpu.VMEM((atoms_dev * nb, width), BF16),
             pltpu.VMEM((edges, width), F32),
             pltpu.VMEM((edges, width), BF16),
@@ -629,15 +653,20 @@
             pltpu.VMEM((edges, width), BF16),
             pltpu.VMEM((edges, width), BF16),
             pltpu.VMEM((NY, NX, NC, 16, 2 * width), BF16),
-            pltpu.VMEM((NY, NX, NC, 16, small), BF16),
+            pltpu.VMEM((NY, NX, NC, 16, 128), BF16),
+            pltpu.VMEM((NY, NX, NC, 16, half), BF16),
             pltpu.VMEM((NY, NX, 16, 2 * width), BF16),
-            pltpu.VMEM((NY, NX, 16, small), BF16),
+            pltpu.VMEM((NY, NX, 16, 128), BF16),
+            pltpu.VMEM((NY, NX, 16, half), BF16),
             pltpu.VMEM((steps, 16, 2 * width), BF16),
-            pltpu.VMEM((steps, 16, small), BF16),
+            pltpu.VMEM((steps, 16, 128), BF16),
+            pltpu.VMEM((steps, 16, half), BF16),
             pltpu.VMEM((steps, 16, 2 * width), BF16),
-            pltpu.VMEM((steps, 16, small), BF16),
+            pltpu.VMEM((steps, 16, 128), BF16),
+            pltpu.VMEM((steps, 16, half), BF16),
             pltpu.VMEM((NX, 2, 16, width), F32),
-            pltpu.VMEM((NX, 16, small), F32),
+            pltpu.VMEM((NX, 16, 128), F32),
+            pltpu.VMEM((NX, 16, half), F32),
             pltpu.VMEM((3, 16, width), BF16),
             pltpu.VMEM((3, 16, width), BF16),
             pltpu.VMEM((3, 16, 128), BF16),
@@ -654,12 +683,12 @@
             dma((NY,)),
             dma((2 * NY,)),
             dma((2 * NY,)),
-            dma((2, NY)),
-            dma((2, NY)),
-            dma((2, steps)),
-            dma((2, steps)),
-            dma((2, steps)),
-            dma((2, steps)),
+            dma((3, NY)),
+            dma((3, NY)),
+            dma((3, steps)),
+            dma((3, steps)),
+            dma((3, steps)),
+            dma((3, steps)),
             dma((3, 3)),
             dma((3, 3)),
             dma((n_dp // 2,)),

time: 74.4 us -> 73.8 us (level)
  no operation moved by 1% of the time
where the time goes in v5:
time: 73.8 us; the launch traced here: 73.5 us
  Pallas kernels  72.3 us (98%)
  between operations  1.29 us (2%)
    pallas_call x1, Pallas kernels, shards(): pl.pallas_call(lambda *refs: kernel(n_dp, *refs), out_shape=(jax.ShapeDty...  70.1 us
    pallas_call x1, Pallas kernels, shards(): pl.pallas_call(write_out, out_shape=(jax.ShapeDtypeStruct((edges, width),...  2.13 us

profile of v5, /device:TPU:2, one launch (start us, length us, event | category | flops | bytes accessed | tf_op | source)
XLA Modules:
  0.0 73.5 jit_solution(5542881485326541617)
XLA Ops:
  1.3 70.1 %shard_map.138 = (bf16[512,1024]{1,0:T(8,128)(2,1)}, bf16[8,1024]{1,0:T(8,128)(2,1)}, f32[32,1024]{1,0:T(8,128)}, f32[16,128]{1,0:T(8,128)}) custom-call(bf16[8,1024]{1,0:T(8,128)(2,1)} %bitcast.9, bf16[512,1024]{1,0:T(8,128)(2,1)} %bitcast.7, s32[1,512]{1,0:T(1,128)} %refs_2_.1, s32[1,512]{1,0:T(1,128)} %refs_3_.1, s32[1,1024]{1,0:T(1,128)} %refs_4_.1, ...), custom_call_target="tpu_custom_call" | custom-call | tf_op jit(solution)/shard_map/pallas_call | solution.py:623
  71.4 2.1 %shard_map.139 = (bf16[512,1024]{1,0:T(8,128)(2,1)}, bf16[8,1024]{1,0:T(8,128)(2,1)}, f32[32,1024]{1,0:T(8,128)}, f32[32,64]{1,0:T(8,128)}) custom-call(bf16[512,1024]{1,0:T(8,128)(2,1)} %get-tuple-element.12.gx, bf16[8,1024]{1,0:T(8,128)(2,1)} %get-tuple-element.13.gh, f32[32,1024]{1,0:T(8,128)} %get-tuple-element.14.gw, f32[16,128]{1,0:T(8,128)} %get-tuple-element.15.gwb), custom_call_target="tpu_custom_call" | custom-call | tf_op jit(solution)/shard_map/pallas_call | solution.py:715

commit v6 on v5

--- a/solution.py
+++ b/solution.py
@@ -539,6 +539,23 @@
     x_out_h[...] = acc_h[1 - xl].astype(BF16)
     begin(x_copy_h)
 
+    x_copy_h.wait_recv()
+    grad_h = acc_h[xl] + x_in_h[...].astype(F32)
+    gh_ref[...] = (
+        cot + jnp.concatenate([grad_h[:atoms_dev], grad_h[atoms_dev:]], axis=1)
+    ).astype(BF16)
+
+    for step in steps_z[:-1]:
+        tile, copy = share(step)
+
+        @pl.when(tile < mine)
+        def _(copy=copy):
+            copy.wait_send()
+
+    for copy in sent:
+        copy.wait_send()
+    store_gx.wait()
+
     @pl.loop(0, 2 * tiles + 1)
     def _(t):
         @pl.when(jnp.logical_or(t != own_tile, z >= mine))
@@ -552,27 +569,10 @@
         gw_ref[r * 16 : (r + 1) * 16, q * 128 : (q + 1) * 128] = dp_all[t].astype(F32)
     gwb_ref[...] = dp_all[2 * tiles].astype(F32)
 
-    x_copy_h.wait_recv()
-    grad_h = acc_h[xl] + x_in_h[...].astype(F32)
-    gh_ref[...] = (
-        cot + jnp.concatenate([grad_h[:atoms_dev], grad_h[atoms_dev:]], axis=1)
-    ).astype(BF16)
-
     @pl.when(z < mine)
     def _():
         for copy in totals:
             copy.wait_send()
-
-    for step in steps_z[:-1]:
-        tile, copy = share(step)
-
-        @pl.when(tile < mine)
-        def _(copy=copy):
-            copy.wait_send()
-
-    for copy in sent:
-        copy.wait_send()
-    store_gx.wait()
 
 
 def write_out(gx, gh, gw, gwb, gx_hbm, gh_hbm, gw_hbm, gwb_hbm, gx_ref, gh_ref, gw_ref, in_ref, out_ref, get, put):

time: 73.8 us -> 73.6 us (level)
  no operation moved by 1% of the time
where the time goes in v6:
time: 73.6 us; the launch traced here: 73.4 us
  Pallas kernels  72.1 us (98%)
  between operations  1.29 us (2%)
    pallas_call x1, Pallas kernels, shards(): pl.pallas_call(lambda *refs: kernel(n_dp, *refs), out_shape=(jax.ShapeDty...  69.9 us
    pallas_call x1, Pallas kernels, shards(): pl.pallas_call(write_out, out_shape=(jax.ShapeDtypeStruct((edges, width),...  2.13 us

profile of v6, /device:TPU:2, one launch (start us, length us, event | category | flops | bytes accessed | tf_op | source)
XLA Modules:
  0.0 73.4 jit_solution(4172260370528959530)
XLA Ops:
  1.3 69.9 %shard_map.138 = (bf16[512,1024]{1,0:T(8,128)(2,1)}, bf16[8,1024]{1,0:T(8,128)(2,1)}, f32[32,1024]{1,0:T(8,128)}, f32[16,128]{1,0:T(8,128)}) custom-call(bf16[8,1024]{1,0:T(8,128)(2,1)} %bitcast.9, bf16[512,1024]{1,0:T(8,128)(2,1)} %bitcast.7, s32[1,512]{1,0:T(1,128)} %refs_2_.1, s32[1,512]{1,0:T(1,128)} %refs_3_.1, s32[1,1024]{1,0:T(1,128)} %refs_4_.1, ...), custom_call_target="tpu_custom_call" | custom-call | tf_op jit(solution)/shard_map/pallas_call | solution.py:623
  71.2 2.1 %shard_map.139 = (bf16[512,1024]{1,0:T(8,128)(2,1)}, bf16[8,1024]{1,0:T(8,128)(2,1)}, f32[32,1024]{1,0:T(8,128)}, f32[32,64]{1,0:T(8,128)}) custom-call(bf16[512,1024]{1,0:T(8,128)(2,1)} %get-tuple-element.12.gx, bf16[8,1024]{1,0:T(8,128)(2,1)} %get-tuple-element.13.gh, f32[32,1024]{1,0:T(8,128)} %get-tuple-element.14.gw, f32[16,128]{1,0:T(8,128)} %get-tuple-element.15.gwb), custom_call_target="tpu_custom_call" | custom-call | tf_op jit(solution)/shard_map/pallas_call | solution.py:715
